TPU v7x, 512 devices: a whole 4x4x16 slice. The times are simulated.
512 devices in a mesh: replica: 32 (over x_lo, z), brick: 16 (over y, x_hi, core).
Axes of the slice: x: 4 (x_hi: 2, x_lo: 2; x = x_hi * 2 + x_lo), y: 4, z: 16, core: 2. Of those that a mesh axis runs over, the one named last changes fastest.
Arguments:
- atom_locations: float32 [32, 3, 12288], P('replica', None, 'brick'), may hold values from 0 to 160, as said below
- atom_speeds_vector: float32 [32, 3, 12288], P('replica', None, 'brick'), may hold values from -7 to 7
- inertial_amounts: float32 [12288], P('brick'), may hold values from 1 to 4
- electric_loads: float32 [12288], P('brick'), may hold values from -4 to 4
- scatter_strengths: float32 [12288], P('brick'), may hold values from 0.5 to 2
- gaussian_spreads_sigma: float32 [12288], P('brick'), may hold values from 0.7 to 1.4
- atom_present_flags: int32 [12288], P('brick'), may hold values 0 or 1
- observed_volume_values: float32 [160, 128, 128], P('brick'), may hold values from 0 to 2
- voxel_reciprocal_spread: float32 [160, 128, 128], P('brick'), may hold values from 0.5 to 4
- paired_partner_lists: int32 [96, 14], P('brick'), may hold values from 0 to 9
- cell_usage_tally: int32 [96], P('brick'), may hold values from 1 to 14, as said below
- halo_sender_spots: int32 [2, 4096], P(None, 'brick'), may hold values from 0 to 767
- target_warmth_levels: int32 [32], P('replica'), may hold values from 280 to 399
Outputs:
- new_positions: float32 [32, 3, 12288], P('replica', None, 'brick')
- new_velocities: float32 [32, 3, 12288], P('replica', None, 'brick')
- deviation: float32 [160, 128, 128], P('brick', 'replica')
Inputs may be any that keep to these rules, and one draw needn't show every extreme that they name: `atom_locations`: atoms in the slots of brick b have x in [b * 10, (b + 1) * 10), y in [0, 128), z in [0, 128). Only the first cell_usage_tally[c] slots of cell c count; some cell uses all 14 slots.
All inputs are finite; a program needn't handle non-finite values. No bound on the sum of `atom_present_flags` on one device may be relied on, other than what follows from the above.
Results may differ from a plain program's by a relative error of at most 0.00062.
Values may be sent and summed in bfloat16 or wider, within the bound.
A program may use at most 64 MiB of HBM per device.

v0:
```python
import jax
import jax.numpy as jnp
from jax import lax
from jax.sharding import PartitionSpec as P

HALO = 2
CELL = 128


restraint = 0.1
coupling = 5.0
softening = 1.0
timestep = 0.5
boltzmann = 0.015
heat_bath_damping = 0.5


def from_behind(block, axis, distance):
    devices = range(lax.axis_size(axis))
    route = [((i - distance) % len(devices), i) for i in devices]
    return lax.ppermute(block, axis, route)


def padded(block, sides, width):
    for axis, dim in sides:
        count = lax.axis_size(axis)
        forward = [(i, i + 1) for i in range(count - 1)]
        forward.append((count - 1, 0))
        backward = [(target, source) for source, target in forward]
        low = lax.ppermute(
            lax.slice_in_dim(block, block.shape[dim] - width, None, axis=dim), axis, forward
        )
        high = lax.ppermute(lax.slice_in_dim(block, 0, width, axis=dim), axis, backward)
        block = jnp.concatenate([low, block, high], axis=dim)
    return block


def wrapped(delta, period):
    return delta - period * jnp.floor(delta / period + 0.5)


def factors(grid, coord, inv_var, period):
    delta = wrapped(grid[:, None] - coord[None, :], period)
    value = jnp.exp(-0.5 * delta * delta * inv_var[None, :])
    return (value, delta * inv_var[None, :] * value)


def spread(x_val, y_val, z_fac, amp):

    def spread_one_plane(row):
        left = ((amp * row)[None, :] * y_val).astype(jnp.bfloat16)
        return lax.dot_general(
            left, z_fac, (((1,), (1,)), ((), ())), preferred_element_type=jnp.float32
        )

    return lax.map(spread_one_plane, x_val)


def map_forces(grad_ext, x_val, x_der, y_val, y_der, z_pair, amp):
    count = amp.shape[0]

    def map_one_plane(carry, inputs):
        plane, x_one, x_slope = inputs
        product = jnp.dot(plane, z_pair, preferred_element_type=jnp.float32)
        along = product[:, :count]
        across = product[:, count:]
        first = jnp.sum(y_val * along, axis=0)
        second = jnp.sum(y_der * along, axis=0)
        third = jnp.sum(y_val * across, axis=0)
        return (carry + jnp.stack([x_slope * first, x_one * second, x_one * third]), None)

    total, _ = lax.scan(map_one_plane, jnp.zeros((3, count), jnp.float32), (grad_ext, x_val, x_der))
    return -amp[None, :] * total


def pair_forces(coords, charge, ghost_low, ghost_high, paired_partner_lists, live, periods, limit):
    own = jnp.concatenate([coords, charge[None, :]], 0).reshape(4, -1, CELL)
    blocks = jnp.concatenate(
        [own, ghost_low.reshape(4, -1, CELL), ghost_high.reshape(4, -1, CELL)], axis=1
    )
    period = jnp.array([float(p) for p in periods], jnp.float32)[:, None, None, None]

    def slot(index, total):
        partner = jnp.take(blocks, paired_partner_lists[:, index], axis=1)
        delta = wrapped(own[:3, :, :, None] - partner[:3, :, None, :], period)
        dist = jnp.sum(delta * delta, axis=0) + softening
        active = (index < live).astype(jnp.float32)
        scale = (
            coupling
            * own[3][:, :, None]
            * partner[3][:, None, :]
            * active[:, None, None]
            / (dist * jnp.sqrt(dist))
        )
        return total + jnp.sum(scale[None] * delta, axis=3)

    total = lax.fori_loop(0, limit, slot, jnp.zeros((3, own.shape[1], CELL), jnp.float32))
    return total.reshape(3, -1)


def local(
    atom_locations,
    atom_speeds_vector,
    inertial_amounts,
    electric_loads,
    scatter_strengths,
    gaussian_spreads_sigma,
    atom_present_flags,
    observed_volume_values,
    voxel_reciprocal_spread,
    paired_partner_lists,
    cell_usage_tally,
    halo_sender_spots,
    target_warmth_levels,
):
    thick, rows, depth = observed_volume_values.shape
    slabs = lax.axis_size("brick")
    members = lax.axis_size("replica")
    brick = lax.axis_index("brick")
    n_x = thick * slabs
    coords = atom_locations[0]
    count = coords.shape[1]
    occupancy = atom_present_flags.astype(jnp.float32)
    amp = occupancy * scatter_strengths
    charge = occupancy * electric_loads
    inv_var = 1.0 / (gaussian_spreads_sigma * gaussian_spreads_sigma)
    planes = thick + 2 * HALO
    plane_grid = (brick * thick - HALO + jnp.arange(planes, dtype=jnp.int32)).astype(jnp.float32)
    x_val, x_der = factors(plane_grid, coords[0], inv_var, n_x)
    y_val, y_der = factors(
        jnp.arange(rows, dtype=jnp.int32).astype(jnp.float32), coords[1], inv_var, rows
    )
    z_val, z_der = factors(
        jnp.arange(depth, dtype=jnp.int32).astype(jnp.float32), coords[2], inv_var, depth
    )
    z_pair = jnp.concatenate([z_val, z_der], axis=1).astype(jnp.bfloat16)
    partial_value = spread(x_val, y_val, z_pair[:, :count], amp)
    packet_up = jnp.concatenate(
        [
            jnp.take(coords, halo_sender_spots[0], axis=1),
            jnp.take(charge, halo_sender_spots[0])[None, :],
        ],
        0,
    )
    packet_down = jnp.concatenate(
        [
            jnp.take(coords, halo_sender_spots[1], axis=1),
            jnp.take(charge, halo_sender_spots[1])[None, :],
        ],
        0,
    )
    rim_low, ghost_low = from_behind((partial_value[thick + HALO :], packet_up), "brick", 1)
    rim_high, ghost_high = from_behind((partial_value[:HALO], packet_down), "brick", -1)
    pad_low = jnp.pad(rim_low, ((0, thick - HALO), (0, 0), (0, 0)))
    pad_high = jnp.pad(rim_high, ((thick - HALO, 0), (0, 0), (0, 0)))
    local_map = partial_value[HALO : HALO + thick] + pad_low + pad_high
    share_rows = rows // members
    start = lax.axis_index("replica") * share_rows
    summed = lax.psum(local_map, "replica")
    whole = summed / members - observed_volume_values
    grad = (restraint * voxel_reciprocal_spread * whole).astype(jnp.bfloat16)
    deviation = lax.dynamic_slice_in_dim(whole, start, share_rows, 1)
    grad_ext = padded(grad, (("brick", 0),), HALO)
    restraint_force = map_forces(grad_ext, x_val, x_der, y_val, y_der, z_pair, amp)
    limit = paired_partner_lists.shape[1]
    short = pair_forces(
        coords,
        charge,
        ghost_low,
        ghost_high,
        paired_partner_lists,
        cell_usage_tally,
        (n_x, rows, depth),
        limit,
    )
    forces = restraint_force + short
    v_half = atom_speeds_vector[0] + timestep * forces / inertial_amounts[None, :]
    kinetic = lax.psum(jnp.sum(inertial_amounts[None, :] * v_half * v_half), "brick")
    present_moment = kinetic / (3 * count * slabs * boltzmann) + 1e-06
    rescale_ratio = jnp.sqrt(
        1.0
        + heat_bath_damping * (target_warmth_levels[0].astype(jnp.float32) / present_moment - 1.0)
    )
    new_velocities = rescale_ratio * v_half
    new_positions = coords + timestep * new_velocities
    return (new_positions[None], new_velocities[None], deviation)


def solution(mesh):
    return jax.shard_map(
        local,
        mesh=mesh,
        in_specs=(
            P("replica", None, "brick"),
            P("replica", None, "brick"),
            P("brick"),
            P("brick"),
            P("brick"),
            P("brick"),
            P("brick"),
            P("brick", None, None),
            P("brick", None, None),
            P("brick", None),
            P("brick"),
            P(None, "brick"),
            P("replica"),
        ),
        out_specs=(
            P("replica", None, "brick"),
            P("replica", None, "brick"),
            P("brick", "replica", None),
        ),
        check_vma=False,
    )
```

profile of v0, /device:TPU:1, one launch (start us, length us, event | category | flops | bytes accessed | tf_op | source)
XLA Modules:
  0.0 368.9 jit_solution(12493634837748243994)
XLA Ops:
  7.2 0.8 fusion.82
  8.7 0.7 fusion.79
  9.4 1.4 gather_fusion.4
  11.0 0.7 gather_fusion.3
  12.0 8.8 %collective-permute-start.5 = (f32[4,256]{1,0:T(4,128)S(1)}, f32[4,256]{1,0:T(4,128)S(1)}, u32[]{:S(2)}, u32[]{:S(2)}) collective-permute-start(f32[4,256]{1,0:T(4,128)S(1)} %pad_maximum_fusion.5), channel_id=1, source_target_pairs={{1,0},{2,1},{3,2},{4,3},{5,4},{6,5},{7,6},{8,7},{9,8},{10,9},{11,1... | collective-permute-start | bytes 12296 | tf_op jit(solution)/shard_map/ppermute | solution.py:21
  20.8 1.4 gather_fusion.2
  22.1 0.7 gather_fusion.1
  23.1 1.9 collective-permute-start.4
  25.2 7.7 %while.40 = (s32[]{:T(128)}, f32[14,128,128]{2,1,0:T(8,128)S(1)}, f32[768]{0:T(1024)S(1)}, f32[14,768]{1,0:T(8,128)S(1)}, f32[768]{0:T(1024)S(1)}, /*index=5*/f3...) while((s32[]{:T(128)}, f32[14,128,128]{2,1,0:T(8,128)S(1)}, ...), condition=%wide.region_1.2_spmd.clone.clone, body=%wide.region_0.1_spmd.clone.clone.sunk | while | flops 27230976 | bytes 96365 | solution.py:56
  33.0 1.9 collective-permute-start
  34.9 2.4 collective-permute-start.1
  38.5 4.4 %collective-permute-done.1 = f32[2,128,128]{2,1,0:T(8,128)S(1)} collective-permute-done((f32[2,128,128]{2,1,0:T(8,128)S(1)}, f32[2,128,128]{2,1,0:T(8,128)S(1)}, u32[]{:S(2)}, u32[]{:S(2)}) %collective-permute-start.1) | collective-permute-done | bytes 131104 | tf_op jit(solution)/shard_map/ppermute | solution.py:21
  43.0 0.9 pad_add_fusion
  44.0 29.7 %while.41 = (s32[]{:T(128)}, f32[3,6,128]{2,1,0:T(8,128)S(1)}, f32[4,6,128]{2,1,0:T(8,128)S(1)}, s32[6,14]{0,1:T(8,128)S(1)}, f32[4,10,128]{2,0,1:T(4,128)S(1)},...) while((s32[]{:T(128)}, f32[3,6,128]{2,1,0:T(8,128)S(1)}, ...), condition=%wide.region_11.14_spmd.clone.clone, body=%wide.region_8.13_spmd.clone.clone.sunk | while | flops 5119027 | bytes 1761635 | solution.py:97
  45.3 0.7 fusion.98
  47.5 0.7 fusion.98
  49.6 0.7 fusion.98
  51.7 0.7 fusion.98
  53.8 0.7 fusion.98
  55.9 0.7 fusion.98
  58.0 0.7 fusion.98
  60.2 0.7 fusion.98
  62.3 0.7 fusion.98
  64.4 0.7 fusion.98
  66.5 0.7 fusion.98
  73.6 208.5 %all-reduce.4.cloned.1.call-done = f32[10,128,128]{2,1,0:T(8,128)} async-done(((f32[10,128,128]{2,1,0:T(8,128)}), f32[10,128,128]{2,1,0:T(8,128)}) %all-reduce.4.cloned.1.call-update) | async-done | bytes 655376 | tf_op jit(solution)/shard_map/psum | solution.py:159
  282.2 1.3 multiply_convert_fusion
  283.5 26.6 %collective-permute-start.2 = (bf16[2,128,128]{2,1,0:T(8,128)(2,1)S(1)}, bf16[2,128,128]{2,1,0:T(8,128)(2,1)S(1)}, u32[]{:S(2)}, u32[]{:S(2)}) collective-permute-start(bf16[2,128,128]{2,1,0:T(8,128)(2,1)S(1)} %get-tuple-element.541), channel_id=1, source_target_pairs={{0,1},{1,2},{2,3},{3,4},{4,5},{5,6},{6,7},{7,8},{8,9},{9,10},{10,1... | collective-permute-start | bytes 196616 | tf_op jit(solution)/shard_map/ppermute | solution.py:30
  310.1 1.9 collective-permute-start.3
  312.6 4.5 %collective-permute-done.3 = bf16[2,128,128]{2,1,0:T(8,128)(2,1)S(1)} collective-permute-done((bf16[2,128,128]{2,1,0:T(8,128)(2,1)S(1)}, bf16[2,128,128]{2,1,0:T(8,128)(2,1)S(1)}, u32[]{:S(2)}, u32[]{:S(2)}) %collective-permute-start.3) | collective-permute-done | bytes 65568 | tf_op jit(solution)/shard_map/ppermute | solution.py:33
  317.3 9.2 %while.42 = (s32[]{:T(128)}, f32[3,768]{1,0:T(4,128)S(1)}, f32[14,768]{1,0:T(8,128)S(1)}, bf16[14,128,128]{2,1,0:T(8,128)(2,1)S(1)}, bf16[128,1536]{1,0:T(8,128)...) while((s32[]{:T(128)}, f32[3,768]{1,0:T(4,128)S(1)}, ...), condition=%wide.region_7.8_spmd.clone.clone.clone, body=%wide.region_3.7_spmd.clone.clone.clone.sunk | while | flops 52012032 | bytes 2067079 | solution.py:72
  327.1 32.9 %psum.15 = f32[]{:T(128)} all-reduce(f32[]{:T(128)} %get-tuple-element.524), channel_id=1, replica_groups=mesh['replica'=32,'brick'=16] {'brick'}, use_global_device_ids=true, to_apply=%region_13.16 | all-reduce | flops 1 | bytes 8 | tf_op jit(solution)/shard_map/psum | solution.py:178
  (316 shorter events, 40.8 us)
Async XLA Ops:
  7.2 275.0 %all-reduce.4.cloned.1.call-start = ((), (), s32[]{:S(2)}) async-start(), calls=%async_computation | async-start | bytes 1310720 | tf_op jit(solution)/shard_map/psum | solution.py:159
  11.7 13.3 %copy-start.2 = (f32[1,3,768]{2,0,1:T(1,128)S(1)}, f32[1,3,768]{2,0,1:T(1,128)}, u32[]{:S(2)}) copy-start(f32[1,3,768]{2,0,1:T(1,128)} %param.24) | copy-start | bytes 27652
  12.0 26.5 %collective-permute-start.5 = (f32[4,256]{1,0:T(4,128)S(1)}, f32[4,256]{1,0:T(4,128)S(1)}, u32[]{:S(2)}, u32[]{:S(2)}) collective-permute-start(f32[4,256]{1,0:T(4,128)S(1)} %pad_maximum_fusion.5), channel_id=1, source_target_pairs={{1,0},{2,1},{3,2},{4,3},{5,4},{6,5},{7,6},{8,7},{9,8},{10,9},{11,1... | collective-permute-start | bytes 12296 | tf_op jit(solution)/shard_map/ppermute | solution.py:21
  23.1 15.4 %collective-permute-start.4 = (f32[4,256]{1,0:T(4,128)S(1)}, f32[4,256]{1,0:T(4,128)S(1)}, u32[]{:S(2)}, u32[]{:S(2)}) collective-permute-start(f32[4,256]{1,0:T(4,128)S(1)} %pad_maximum_fusion.4), channel_id=1, source_target_pairs={{15,0},{0,1},{1,2},{2,3},{3,4},{4,5},{5,6},{6,7},{7,8},{8,9},{9,10... | collective-permute-start | bytes 12296 | tf_op jit(solution)/shard_map/ppermute | solution.py:21
  32.9 5.4 %copy-start.6 = (s32[6,14]{1,0:T(8,128)S(1)}, s32[6,14]{1,0:T(8,128)}, u32[]{:S(2)}) copy-start(s32[6,14]{1,0:T(8,128)} %param.33) | copy-start | bytes 1012
  33.0 5.6 %collective-permute-start = (f32[2,128,128]{2,1,0:T(8,128)S(1)}, f32[2,128,128]{2,1,0:T(8,128)S(1)}, u32[]{:S(2)}, u32[]{:S(2)}) collective-permute-start(f32[2,128,128]{2,1,0:T(8,128)S(1)} %get-tuple-element.539), channel_id=1, source_target_pairs={{15,0},{0,1},{1,2},{2,3},{3,4},{4,5},{5,6},{6,7},{7,8},{8,9},{9,10... | collective-permute-start | bytes 393224 | tf_op jit(solution)/shard_map/ppermute | solution.py:21
  34.9 8.1 %collective-permute-start.1 = (f32[2,128,128]{2,1,0:T(8,128)S(1)}, f32[2,128,128]{2,1,0:T(8,128)S(1)}, u32[]{:S(2)}, u32[]{:S(2)}) collective-permute-start(f32[2,128,128]{2,1,0:T(8,128)S(1)} %get-tuple-element.540), channel_id=1, source_target_pairs={{1,0},{2,1},{3,2},{4,3},{5,4},{6,5},{7,6},{8,7},{9,8},{10,9},{11,1... | collective-permute-start | bytes 393224 | tf_op jit(solution)/shard_map/ppermute | solution.py:21
  38.5 5.4 %copy-start.3 = (f32[3]{0:T(128)S(1)}, f32[3]{0:T(128)}, u32[]{:S(2)}) copy-start(f32[3]{0:T(128)} %constant.342) | copy-start | bytes 40
  38.5 5.4 %copy-start.4 = (f32[3]{0:T(128)S(1)}, f32[3]{0:T(128)}, u32[]{:S(2)}) copy-start(f32[3]{0:T(128)} %constant.341) | copy-start | bytes 40
  38.5 5.4 %copy-start.8 = (s32[6]{0:T(128)S(1)}, s32[6]{0:T(128)}, u32[]{:S(2)}) copy-start(s32[6]{0:T(128)} %param.34) | copy-start | bytes 76
  43.9 238.2 %copy-start = (f32[10,128,128]{2,1,0:T(8,128)S(1)}, f32[10,128,128]{2,1,0:T(8,128)}, u32[]{:S(2)}) copy-start(f32[10,128,128]{2,1,0:T(8,128)} %param.32) | copy-start | bytes 1966084
  44.0 238.2 %copy-start.1 = (f32[10,128,128]{2,1,0:T(8,128)S(1)}, f32[10,128,128]{2,1,0:T(8,128)}, u32[]{:S(2)}) copy-start(f32[10,128,128]{2,1,0:T(8,128)} %param.31) | copy-start | bytes 1966084
  283.5 29.2 %collective-permute-start.2 = (bf16[2,128,128]{2,1,0:T(8,128)(2,1)S(1)}, bf16[2,128,128]{2,1,0:T(8,128)(2,1)S(1)}, u32[]{:S(2)}, u32[]{:S(2)}) collective-permute-start(bf16[2,128,128]{2,1,0:T(8,128)(2,1)S(1)} %get-tuple-element.541), channel_id=1, source_target_pairs={{0,1},{1,2},{2,3},{3,4},{4,5},{5,6},{6,7},{7,8},{8,9},{9,10},{10,1... | collective-permute-start | bytes 196616 | tf_op jit(solution)/shard_map/ppermute | solution.py:30
  310.1 7.1 %collective-permute-start.3 = (bf16[2,128,128]{2,1,0:T(8,128)(2,1)S(1)}, bf16[2,128,128]{2,1,0:T(8,128)(2,1)S(1)}, u32[]{:S(2)}, u32[]{:S(2)}) collective-permute-start(bf16[2,128,128]{2,1,0:T(8,128)(2,1)S(1)} %get-tuple-element.542), channel_id=1, source_target_pairs={{1,0},{2,1},{3,2},{4,3},{5,4},{6,5},{7,6},{8,7},{9,8},{10,9},{11,1... | collective-permute-start | bytes 196616 | tf_op jit(solution)/shard_map/ppermute | solution.py:33
  317.2 9.2 %copy-start.5 = (f32[1,3,768]{2,0,1:T(1,128)S(1)}, f32[1,3,768]{2,0,1:T(1,128)}, u32[]{:S(2)}) copy-start(f32[1,3,768]{2,0,1:T(1,128)} %param.25) | copy-start | bytes 27652
  317.2 9.2 %copy-start.7 = (f32[768]{0:T(1024)S(1)}, f32[768]{0:T(1024)}, u32[]{:S(2)}) copy-start(f32[768]{0:T(1024)} %param.26) | copy-start | bytes 9220
Sparse Core Ops, SparseCore 0:
  44.0 238.0 all-reduce.3
where the time goes:
time: 374 us; the launch traced here: 369 us
  waiting for transfers between devices  218 us (58%)
  starting transfers between devices  43.6 us (12%)
  blocking collectives  32.9 us (9%)
  other arithmetic  30 us (8%)
  local copies, waits for them, and re-layouts  16.3 us (4%)
  between operations  15.8 us (4%)
  matrix products  10.4 us (3%)
    psum x1, waiting for transfers between devices, local(): summed = lax.psum(local_map, 'replica')  209 us
    psum x1, blocking collectives, local(): lax.psum(jnp.sum(inertial_amounts[None, :] * v_half * v_half), 'brick')  32.9 us
    ppermute x1, starting transfers between devices, padded(): lax.ppermute(lax.slice_in_dim(block, block.shape[dim] - width, None, axis...  26.6 us
    ppermute x4, starting transfers between devices, from_behind(): return lax.ppermute(block, axis, route)  15 us
    reduce_sum x14, other arithmetic, slot(): return total + jnp.sum(scale[None] * delta, axis=3)  10.2 us
    gather x14, local copies, waits for them, and re-layouts, slot(): partner = jnp.take(blocks, paired_partner_lists[:, index], axis=1)  8.02 us
  transfers between devices with their start and end apart: 7, of which 3 were waited for; matrix products, arithmetic and copies ran while one was open for 11% of the time, Pallas kernels for 0%

commit v1 on v0

v1 whole, which is shorter than its diff:
```python
import functools
import math

import jax
import jax.numpy as jnp
from jax import lax
from jax.experimental import pallas as pl
from jax.experimental.pallas import tpu as pltpu
from jax.sharding import PartitionSpec as P

MESH = pl.DeviceIdType.MESH

HALO = 2
CELL = 128
GHOST = 256
LOG2E = 1.4426950408889634

restraint = 0.1
coupling = 5.0
softening = 1.0
timestep = 0.5
boltzmann = 0.015
heat_bath_damping = 0.5

B_STEPS = ((0, 0), (0, 1), (1, 0), (1, 1))


def fixed(coord, period):
    scale = 2.0**31 / period
    return (coord * scale).astype(jnp.int32) << 1


def dot_t(a, b):
    return lax.dot_general(a, b, (((1,), (1,)), ((), ())), preferred_element_type=jnp.float32)


def kernel(
    dims,
    loc,
    vel,
    mass_ref,
    load_ref,
    strength_ref,
    sigma_ref,
    flag_ref,
    spots,
    lists,
    tally,
    warm,
    obs,
    vrs,
    pos_out,
    vel_out,
    dev_out,
    crd,
    zz,
    gxs,
    gxds,
    gys,
    gyds,
    acc,
    rs,
    lo,
    hi,
    obst,
    vrst,
    grd,
    frc,
    frcin,
    gsend,
    glo,
    ghi,
    bx,
    bq,
    by,
    bz,
    colx,
    coly,
    colz,
    pacc,
    kin,
    loc_sem,
    crd_ss,
    crd_rs,
    gh_ss,
    gh_rs,
    ob_ss,
    ob_rs,
    rs_ss,
    rs_rs,
    lo_ss,
    lo_rs,
    hi_ss,
    hi_rs,
    gr_ss,
    gr_rs,
    fr_ss,
    fr_rs,
    kn_ss,
    kn_rs,
):
    members, bricks, thick, rows, depth, atoms = dims
    half = members // 2
    na = half // 2
    planes = thick + 2 * HALO
    wide = planes * 8
    cells = atoms // CELL
    slots = lists.shape[1]
    r = lax.axis_index("replica")
    b = lax.axis_index("brick")
    x, z = r // half, r % half
    zh, zp = z // 2, z % 2
    up, down = (b + 1) % bricks, (b + bricks - 1) % bricks

    def a_peer(d):
        return (x * half + ((zh + d) % na) * 2 + zp, b)

    def b_rep(k):
        dx, dp = B_STEPS[k]
        return ((x + dx) % 2) * half + zh * 2 + (zp + dp) % 2

    barrier = pltpu.get_barrier_semaphore()
    partners = [a_peer(d) for d in range(1, na)]
    partners += [(b_rep(k), b) for k in range(1, 4)]
    partners += [(b_rep(k), n) for k in range(1, 4) for n in (up, down)]
    partners += [(r, (b + d) % bricks) for d in range(1, bricks)]
    for p in partners:
        pl.semaphore_signal(barrier, inc=1, device_id=p, device_id_type=MESH)

    row0 = pl.multiple_of(x * (rows // 2) + zh * 8, 8)
    tile = pl.ds(row0, 8)
    local_copies = [
        pltpu.make_async_copy(src.at[:, tile, :], dst.at[pl.ds(HALO, thick)], loc_sem.at[i])
        for i, (src, dst) in enumerate(((obs, obst), (vrs, vrst)))
    ]
    for c in local_copies:
        c.start()
    occ = flag_ref[...].astype(jnp.float32)
    amp = occ * strength_ref[...]
    q = occ * load_ref[...]
    sigma = sigma_ref[...]
    iv = 1.0 / (sigma * sigma)
    for i in range(3):
        crd[0, i] = loc[0, i : i + 1, :]

    sends = []

    def remote(src, dst, ss, rsem, device):
        c = pltpu.make_async_remote_copy(
            src_ref=src, dst_ref=dst, send_sem=ss, recv_sem=rsem, device_id=device, device_id_type=MESH
        )
        c.start()
        sends.append(c)
        return c

    near = []
    for t in range(1, na):
        near.append((t + 1) // 2 if t % 2 else na - t // 2)

    pl.semaphore_wait(barrier, len(partners))
    crd_in = {}
    for d in reversed(near):
        crd_in[d] = remote(crd.at[0], crd.at[d], crd_ss.at[d], crd_rs.at[d], a_peer(d))
    ob_in = []
    for i, (src, dst) in enumerate(((obs, obst), (vrs, vrst))):
        ob_in.append(
            remote(
                src.at[pl.ds(thick - HALO, HALO), tile, :],
                dst.at[pl.ds(0, HALO)],
                ob_ss.at[2 * i],
                ob_rs.at[2 * i],
                (r, up),
            )
        )
        ob_in.append(
            remote(
                src.at[pl.ds(0, HALO), tile, :],
                dst.at[pl.ds(thick + HALO, HALO)],
                ob_ss.at[2 * i + 1],
                ob_rs.at[2 * i + 1],
                (r, down),
            )
        )

    four = jnp.concatenate([loc[0], q], axis=0)
    first = four.astype(jnp.bfloat16).astype(jnp.float32)
    rest = four - first
    second = rest.astype(jnp.bfloat16).astype(jnp.float32)
    third = rest - second
    pieces = jnp.concatenate([first, second, third, jnp.zeros_like(four)], axis=0).astype(jnp.bfloat16)
    slot_of = lax.broadcasted_iota(jnp.int32, (atoms, GHOST), 0)
    gh_in = []
    for side, (dst, device) in enumerate(((glo, (r, up)), (ghi, (r, down)))):
        chosen = jnp.where(slot_of == spots[side : side + 1, :], 1.0, 0.0).astype(jnp.bfloat16)
        got = jnp.dot(pieces, chosen, preferred_element_type=jnp.float32)
        got = got[0:4] + got[4:8] + got[8:12]
        for i in range(4):
            gsend[side, i] = got[i : i + 1]
        gh_in.append(remote(gsend.at[side], dst, gh_ss.at[side], gh_rs.at[side], device))

    shift_y, shift_z = 32 - int(math.log2(rows)), 32 - int(math.log2(depth))
    unit_y, unit_z = 2.0**-shift_y, 2.0**-shift_z
    ivc = iv * (-0.5 * LOG2E)
    plane_at = (b * thick - HALO + lax.broadcasted_iota(jnp.int32, (16, atoms), 0)).astype(jnp.float32)
    row_in = lax.broadcasted_iota(jnp.int32, (16, atoms), 0)
    row_at = (zh * 8 + (row_in // 8) * (rows // 2) + row_in % 8) << shift_y

    def spread(d, start):
        dx = plane_at - crd[d, 0]
        gx = jnp.exp2(dx * dx * ivc)
        gxs[d] = gx
        gxds[d] = dx * iv * gx
        dy = (row_at - fixed(crd[d, 1], rows)).astype(jnp.float32)
        gy = jnp.exp2(dy * dy * (ivc * unit_y**2))
        gys[d] = gy
        gyds[d] = dy * (iv * unit_y) * gy
        level = lax.broadcasted_iota(jnp.int32, (depth, atoms), 0) << shift_z
        dz = (level - fixed(crd[d, 2], depth)).astype(jnp.float32)
        gz = jnp.exp2(dz * dz * (ivc * unit_z**2))
        zz[d, :, atoms:] = (dz * (iv * unit_z) * gz).astype(jnp.bfloat16)
        gzb = gz.astype(jnp.bfloat16)
        zz[d, :, :atoms] = gzb
        ax = (amp * gx)[:planes]
        for t in range(2):
            left = ax[:, None, :] * gy[None, 8 * t : 8 * t + 8, :]
            part = dot_t(left.reshape(wide, atoms).astype(jnp.bfloat16), gzb)
            if start:
                acc[t] = part
            else:
                acc[t] += part

    spread(0, True)

    for c in range(cells):
        at = slice(c * CELL, (c + 1) * CELL)
        for i, col in enumerate((colx, coly, colz)):
            v = jnp.broadcast_to(loc[0, i : i + 1, at], (CELL, CELL)).T
            col[at] = v * 2.0**shift_z if i == 0 else fixed(v, (rows, depth)[i - 1])

    for t, d in enumerate(near):
        crd_in[d].wait_recv()
        spread(d, False)

    rs_in, lo_in, hi_in = [], [], []
    edge = 2 * HALO * 8
    for k in (3, 2, 1, 0):
        dx, dp = B_STEPS[k]
        t = (x + dx) % 2
        if k:
            rs_in.append(remote(acc.at[t], rs.at[k - 1], rs_ss.at[k], rs_rs.at[k], (b_rep(k), b)))
        lo_in.append(
            remote(acc.at[t, pl.ds(wide - edge, edge)], lo.at[k], lo_ss.at[k], lo_rs.at[k], (b_rep(k), up))
        )
        hi_in.append(remote(acc.at[t, pl.ds(0, edge)], hi.at[k], hi_ss.at[k], hi_rs.at[k], (b_rep(k), down)))

    scale_x = 2.0**shift_z
    for c in range(cells):
        at = slice(c * CELL, (c + 1) * CELL)
        bx[c] = loc[0, 0:1, at] * scale_x
        by[c] = fixed(loc[0, 1:2, at], rows)
        bz[c] = fixed(loc[0, 2:3, at], depth)
        bq[c] = q[:, at]
    zero = jnp.zeros((1, CELL), jnp.float32)
    none = cells + 4
    bx[none] = zero
    bq[none] = zero
    by[none] = jnp.zeros((1, CELL), jnp.int32)
    bz[none] = jnp.zeros((1, CELL), jnp.int32)
    for c in gh_in:
        c.wait_recv()
    period_x = float(thick * bricks)
    for side, src in enumerate((glo, ghi)):
        if side == 0:
            move = jnp.where(b == 0, -period_x, 0.0)
        else:
            move = jnp.where(b == bricks - 1, period_x, 0.0)
        for g in range(2):
            at = slice(g * CELL, (g + 1) * CELL)
            n = cells + 2 * side + g
            bx[n] = (src[0, :, at] + move) * scale_x
            by[n] = fixed(src[1, :, at], rows)
            bz[n] = fixed(src[2, :, at], depth)
            bq[n] = src[3, :, at]

    part_rows = 32
    parts = CELL // part_rows

    def pair(u, _):
        c = u // parts
        at = pl.ds(pl.multiple_of(u * part_rows, part_rows), part_rows)
        xi, yi, zi = colx[at], coly[at], colz[at]
        total = [jnp.zeros((part_rows, CELL), jnp.float32)] * 3
        for s in range(slots):
            n = jnp.where(s < tally[0, c], lists[c, s], none)
            dx = xi - bx[n]
            dy = (yi - by[n]).astype(jnp.float32)
            dz = (zi - bz[n]).astype(jnp.float32)
            if shift_y != shift_z:
                dy = dy * 2.0 ** (shift_z - shift_y)
            inv = lax.rsqrt(dx * dx + dy * dy + dz * dz + softening * 4.0**shift_z)
            pull = inv * inv * inv * bq[n]
            total = [total[0] + pull * dx, total[1] + pull * dy, total[2] + pull * dz]
        for i in range(3):
            pacc[i, at] = total[i]
        return 0

    units = cells * parts
    lax.fori_loop(0, units // 3, pair, 0)

    for c in local_copies:
        c.wait()
    for c in ob_in + rs_in + lo_in + hi_in:
        c.wait_recv()
    total = acc[x] + rs[0] + rs[1] + rs[2]
    low = lo[0] + lo[1] + lo[2] + lo[3]
    high = hi[0] + hi[1] + hi[2] + hi[3]
    total = jnp.concatenate(
        [total[:edge] + low, total[edge : wide - edge], total[wide - edge :] + high], axis=0
    )
    dev = total.reshape(planes, 8, depth) / members - obst[...]
    grad = (restraint * vrst[...] * dev).astype(jnp.bfloat16)
    grd[x] = grad.reshape(wide, depth)
    gr_in = remote(grd.at[x], grd.at[x], gr_ss.at[0], gr_rs.at[0], (b_rep(2), b))
    own = dev[HALO : HALO + thick]
    dev_out[...] = jnp.where(zp == 0, own[:, :4], own[:, 4:])

    lax.fori_loop(units // 3, 2 * units // 3, pair, 0)
    gr_in.wait_recv()

    lanes = 256

    def force(d):
        for c in range(atoms // lanes):
            at = slice(c * lanes, (c + 1) * lanes)
            after = slice(atoms + c * lanes, atoms + (c + 1) * lanes)
            f = [0.0, 0.0, 0.0]
            for t in range(2):
                along = jnp.dot(grd[t], zz[d, :, at], preferred_element_type=jnp.float32)
                across = jnp.dot(grd[t], zz[d, :, after], preferred_element_type=jnp.float32)
                sums = [0.0, 0.0, 0.0]
                for i in range(planes):
                    p = along[8 * i : 8 * i + 8]
                    g = gxs[d, i : i + 1, at]
                    sums[0] += gxds[d, i : i + 1, at] * p
                    sums[1] += g * p
                    sums[2] += g * across[8 * i : 8 * i + 8]
                y = gys[d, 8 * t : 8 * t + 8, at]
                f[0] += y * sums[0]
                f[1] += gyds[d, 8 * t : 8 * t + 8, at] * sums[1]
                f[2] += y * sums[2]
            for i in range(3):
                frc[d, i, :, at] = jnp.sum(f[i], axis=0, keepdims=True)

    fr_in = []
    for d in reversed(near):
        force(d)
        fr_in.append(remote(frc.at[d], frcin.at[d], fr_ss.at[d], fr_rs.at[d], a_peer(na - d)))
    force(0)

    lax.fori_loop(2 * units // 3, units, pair, 0)
    short = []
    gain = coupling * 4.0**shift_z
    for i in range(3):
        line = [
            jnp.sum(pacc[i, c * CELL : (c + 1) * CELL].T, axis=0, keepdims=True) for c in range(cells)
        ]
        short.append((gain * q) * jnp.concatenate(line, axis=1))

    for c in fr_in:
        c.wait_recv()
    mass = mass_ref[...]
    v_half = []
    square = jnp.zeros((1, atoms), jnp.float32)
    for i in range(3):
        f = frc[0, i]
        for d in range(1, na):
            f = f + frcin[d, i]
        v = vel[0, i : i + 1, :] + timestep * (short[i] - amp * f) / mass
        square = square + mass * v * v
        v_half.append(v)
    row = square[:, :CELL]
    for c in range(1, cells):
        row = row + square[:, c * CELL : (c + 1) * CELL]
    kin[0] = row
    kn_in = [
        remote(kin.at[0], kin.at[d], kn_ss.at[d], kn_rs.at[d], (r, (b + d) % bricks))
        for d in range(1, bricks)
    ]
    for c in kn_in:
        c.wait_recv()
    for d in range(1, bricks):
        row = row + kin[d]
    kinetic = jnp.sum(row, axis=1, keepdims=True)
    present = kinetic / (3 * atoms * bricks * boltzmann) + 1e-06
    wanted = jnp.full((1, 1), warm[0, 0].astype(jnp.float32))
    ratio = jnp.sqrt(1.0 + heat_bath_damping * (wanted / present - 1.0))
    for i in range(3):
        v = ratio * v_half[i]
        vel_out[0, i : i + 1, :] = v
        pos_out[0, i : i + 1, :] = loc[0, i : i + 1, :] + timestep * v
    for c in sends:
        c.wait_send()


def local(
    atom_locations,
    atom_speeds_vector,
    inertial_amounts,
    electric_loads,
    scatter_strengths,
    gaussian_spreads_sigma,
    atom_present_flags,
    observed_volume_values,
    voxel_reciprocal_spread,
    paired_partner_lists,
    cell_usage_tally,
    halo_sender_spots,
    target_warmth_levels,
):
    thick, rows, depth = observed_volume_values.shape
    atoms = atom_locations.shape[2]
    members, bricks = lax.axis_size("replica"), lax.axis_size("brick")
    na = members // 4
    planes = thick + 2 * HALO
    wide = planes * 8
    cells = atoms // CELL
    blocks = cells + 5
    f32, bf16, i32 = jnp.float32, jnp.bfloat16, jnp.int32
    vmem = pl.BlockSpec(memory_space=pltpu.VMEM)
    smem = pl.BlockSpec(memory_space=pltpu.SMEM)
    anywhere = pl.BlockSpec(memory_space=pl.ANY)
    edge = 2 * HALO * 8
    scratch = [
        pltpu.VMEM((na, 3, 1, atoms), f32),
        pltpu.VMEM((na, depth, 2 * atoms), bf16),
        pltpu.VMEM((na, 16, atoms), f32),
        pltpu.VMEM((na, 16, atoms), f32),
        pltpu.VMEM((na, 16, atoms), f32),
        pltpu.VMEM((na, 16, atoms), f32),
        pltpu.VMEM((2, wide, depth), f32),
        pltpu.VMEM((3, wide, depth), f32),
        pltpu.VMEM((4, edge, depth), f32),
        pltpu.VMEM((4, edge, depth), f32),
        pltpu.VMEM((planes, 8, depth), f32),
        pltpu.VMEM((planes, 8, depth), f32),
        pltpu.VMEM((2, wide, depth), bf16),
        pltpu.VMEM((na, 3, 1, atoms), f32),
        pltpu.VMEM((na, 3, 1, atoms), f32),
        pltpu.VMEM((2, 4, 1, GHOST), f32),
        pltpu.VMEM((4, 1, GHOST), f32),
        pltpu.VMEM((4, 1, GHOST), f32),
        pltpu.VMEM((blocks, 1, CELL), f32),
        pltpu.VMEM((blocks, 1, CELL), f32),
        pltpu.VMEM((blocks, 1, CELL), i32),
        pltpu.VMEM((blocks, 1, CELL), i32),
        pltpu.VMEM((atoms, CELL), f32),
        pltpu.VMEM((atoms, CELL), i32),
        pltpu.VMEM((atoms, CELL), i32),
        pltpu.VMEM((3, atoms, CELL), f32),
        pltpu.VMEM((bricks, 1, CELL), f32),
        pltpu.SemaphoreType.DMA((2,)),
    ]
    for count in (na, 2, 4, 4, 4, 4, 1, na, bricks):
        scratch += [pltpu.SemaphoreType.DMA((count,))] * 2
    flat = lambda v: v.reshape(1, -1)
    return pl.pallas_call(
        functools.partial(kernel, (members, bricks, thick, rows, depth, atoms)),
        out_shape=(
            jax.ShapeDtypeStruct((1, 3, atoms), f32),
            jax.ShapeDtypeStruct((1, 3, atoms), f32),
            jax.ShapeDtypeStruct((thick, rows // members, depth), f32),
        ),
        in_specs=[vmem] * 8 + [smem] * 3 + [anywhere] * 2,
        out_specs=(vmem, vmem, vmem),
        scratch_shapes=scratch,
        compiler_params=pltpu.CompilerParams(
            collective_id=0, has_side_effects=True, vmem_limit_bytes=40 * 2**20
        ),
        cost_estimate=pl.CostEstimate(
            flops=1_200_000_000, bytes_accessed=400_000, transcendentals=4_000_000
        ),
    )(
        atom_locations,
        atom_speeds_vector,
        flat(inertial_amounts),
        flat(electric_loads),
        flat(scatter_strengths),
        flat(gaussian_spreads_sigma),
        flat(atom_present_flags),
        halo_sender_spots,
        paired_partner_lists,
        flat(cell_usage_tally),
        flat(target_warmth_levels),
        observed_volume_values,
        voxel_reciprocal_spread,
    )


def solution(mesh):
    return jax.shard_map(
        local,
        mesh=mesh,
        in_specs=(
            P("replica", None, "brick"),
            P("replica", None, "brick"),
            P("brick"),
            P("brick"),
            P("brick"),
            P("brick"),
            P("brick"),
            P("brick", None, None),
            P("brick", None, None),
            P("brick", None),
            P("brick"),
            P(None, "brick"),
            P("replica"),
        ),
        out_specs=(
            P("replica", None, "brick"),
            P("replica", None, "brick"),
            P("brick", "replica", None),
        ),
        check_vma=False,
    )
```

time: 374 us -> 55.8 us (0.15); the launches traced: 369 us -> 55.4 us
  waiting for transfers between devices: 218 us -> 0 us
  Pallas kernels: 0 us -> 46.6 us
  starting transfers between devices: 43.6 us -> 0 us
  blocking collectives: 32.9 us -> 0 us
  other arithmetic: 30 us -> 0 us
  between operations: 15.8 us -> 1.36 us
  matrix products: 10.4 us -> 0 us
  local copies, waits for them, and re-layouts: 16.3 us -> 7.43 us
    psum x1 -> x0, waiting for transfers between devices: 209 us -> none  [local(): summed = lax.psum(local_map, 'replica')]
    pallas_call x0 -> x1, Pallas kernels: none -> 46.6 us  [local(): pl.pallas_call(functools.partial(kernel, (members, bricks, thick, rows, d...]
    ppermute x6 -> x0, starting transfers between devices: 43.6 us -> none  [the longest x1 26.6 us: padded(): lax.ppermute(lax.slice_in_dim(block, block.shape[dim] - width, None, axis...]
    psum x1 -> x0, blocking collectives: 32.9 us -> none  [local(): lax.psum(jnp.sum(inertial_amounts[None, :] * v_half * v_half), 'brick')]
    reduce_sum x43 -> x0, other arithmetic: 20.8 us -> none  [the longest x14 10.2 us: slot(): return total + jnp.sum(scale[None] * delta, axis=3)]
    gather x18 -> x0, local copies, waits for them, and re-layouts: 12.2 us -> none  [the longest x14 8.02 us: slot(): partner = jnp.take(blocks, paired_partner_lists[:, index], axis=1)]
    dot_general x28 -> x0, matrix products: 10.4 us -> none  [the longest x14 7.01 us: spread_one_plane(): lax.dot_general(left, z_fac, (((1,), (1,)), ((), ())), preferred_element_...]
    ppermute x6 -> x0, waiting for transfers between devices: 8.99 us -> none  [the longest x1 4.53 us: padded(): lax.ppermute(lax.slice_in_dim(block, 0, width, axis=dim), axis, backward)]
  transfers between devices with their start and end apart: 7 -> 0, of which waited for: 3 -> 0; matrix products, arithmetic and copies ran while one was open for 11% -> 0% of each run, Pallas kernels for 0% -> 0%
where the time goes in v1:
time: 55.8 us; the launch traced here: 55.4 us
  Pallas kernels  46.6 us (84%)
  local copies, waits for them, and re-layouts  7.43 us (13%)
  between operations  1.36 us (2%)
    pallas_call x1, Pallas kernels, local(): pl.pallas_call(functools.partial(kernel, (members, bricks, thick, rows, d...  46.6 us
    unnamed x27, local copies, waits for them, and re-layouts  6.2 us
    pallas_call x2, local copies, waits for them, and re-layouts, local(): pl.pallas_call(functools.partial(kernel, (members, bricks, thick, rows, d...  1.22 us

profile of v1, /device:TPU:1, one launch (start us, length us, event | category | flops | bytes accessed | tf_op | source)
XLA Modules:
  0.0 55.4 jit_solution(800247953829529433)
XLA Ops:
  0.6 0.0 copy-start.7
  1.3 0.0 copy-start.8
  1.3 0.0 copy-done.7
  1.3 0.7 %copy-done.8 = f32[768]{0:T(1024)S(1)} copy-done((f32[768]{0:T(1024)S(1)}, f32[768]{0:T(1024)}, u32[]{:S(2)}) %copy-start.8) | copy-done | bytes 3096
  2.0 0.0 copy-start.9
  2.0 0.0 copy-start.10
  2.0 0.7 %copy-done.9 = f32[768]{0:T(1024)S(1)} copy-done((f32[768]{0:T(1024)S(1)}, f32[768]{0:T(1024)}, u32[]{:S(2)}) %copy-start.9) | copy-done | bytes 3096
  2.7 0.0 copy-start.5
  2.7 0.0 copy-done.10
  2.7 0.0 copy-start.11
  2.7 0.7 %copy-done.11 = s32[768]{0:T(1024)S(1)} copy-done((s32[768]{0:T(1024)S(1)}, s32[768]{0:T(1024)}, u32[]{:S(2)}) %copy-start.11) | copy-done | bytes 3096
  3.4 0.0 copy-done.5
  3.4 0.0 copy-start.6
  3.4 0.7 %copy-done.6 = f32[1,3,768]{2,0,1:T(1,128)S(1)} copy-done((f32[1,3,768]{2,0,1:T(1,128)S(1)}, f32[1,3,768]{2,0,1:T(1,128)}, u32[]{:S(2)}) %copy-start.6) | copy-done | bytes 9240
  4.1 0.0 copy-start.2
  4.1 0.0 copy-start.3
  4.1 0.0 copy-start.4
  4.1 0.7 %copy-done.2 = s32[6,14]{1,0:T(8,128)S(1)} copy-done((s32[6,14]{1,0:T(8,128)S(1)}, s32[6,14]{1,0:T(8,128)}, u32[]{:S(2)}) %copy-start.2) | copy-done | bytes 360
  4.8 0.0 copy-done.3
  4.8 0.0 copy-done.4
  4.8 0.0 copy-start
  4.8 1.1 %copy-done = f32[10,128,128]{2,1,0:T(8,128)S(1)} copy-done((f32[10,128,128]{2,1,0:T(8,128)S(1)}, f32[10,128,128]{2,1,0:T(8,128)}, u32[]{:S(2)}) %copy-start) | copy-done | bytes 655384
  5.9 0.0 copy-start.1
  5.9 1.1 %copy-done.1 = f32[10,128,128]{2,1,0:T(8,128)S(1)} copy-done((f32[10,128,128]{2,1,0:T(8,128)S(1)}, f32[10,128,128]{2,1,0:T(8,128)}, u32[]{:S(2)}) %copy-start.1) | copy-done | bytes 655384
  7.0 46.6 %shard_map.148 = (f32[1,3,768]{2,1,0:T(4,128)S(1)}, f32[1,3,768]{2,1,0:T(4,128)S(1)}, f32[10,4,128]{2,1,0:T(4,128)S(1)}) custom-call(f32[1,3,768]{2,1,0:T(4,128)S(1)} %copy.16.loc, f32[1,3,768]{2,1,0:T(4,128)S(1)} %copy.17.vel, f32[1,768]{1,0:T(1,128)S(1)} %reshape.27.mass_ref, f32[1,768]{1,0:T(1,128)S(1)} %reshape.28.load_ref, ...), custom_call_target="tpu_custom_call" | custom-call | flops 1200000000 | bytes 400000 | tf_op jit(solution)/shard_map/pallas_call | solution.py:466
  53.6 0.6 %copy.18 = f32[1,3,768]{2,0,1:T(1,128)} copy(f32[1,3,768]{2,1,0:T(4,128)S(1)} %get-tuple-element.3) | data formatting | bytes 18432 | tf_op jit(solution)/shard_map/pallas_call | solution.py:466
  54.2 0.6 %copy.19 = f32[1,3,768]{2,0,1:T(1,128)} copy(f32[1,3,768]{2,1,0:T(4,128)S(1)} %get-tuple-element.4) | data formatting | bytes 18432 | tf_op jit(solution)/shard_map/pallas_call | solution.py:466
  54.8 0.6 %copy.22 = f32[10,4,128]{2,1,0:T(4,128)} copy(f32[10,4,128]{2,1,0:T(4,128)S(1)} %get-tuple-element.11) | data formatting | bytes 40960
  (7 shorter events, 0.0 us)
Async XLA Ops:
  0.6 0.7 %copy-start.7 = (f32[768]{0:T(1024)S(1)}, f32[768]{0:T(1024)}, u32[]{:S(2)}) copy-start(f32[768]{0:T(1024)} %param.15) | copy-start | bytes 9220
  1.3 0.7 %copy-start.8 = (f32[768]{0:T(1024)S(1)}, f32[768]{0:T(1024)}, u32[]{:S(2)}) copy-start(f32[768]{0:T(1024)} %param.16) | copy-start | bytes 9220
  2.0 0.7 %copy-start.9 = (f32[768]{0:T(1024)S(1)}, f32[768]{0:T(1024)}, u32[]{:S(2)}) copy-start(f32[768]{0:T(1024)} %param.17) | copy-start | bytes 9220
  2.0 0.7 %copy-start.10 = (f32[768]{0:T(1024)S(1)}, f32[768]{0:T(1024)}, u32[]{:S(2)}) copy-start(f32[768]{0:T(1024)} %param.18) | copy-start | bytes 9220
  2.7 0.7 %copy-start.5 = (f32[1,3,768]{2,0,1:T(1,128)S(1)}, f32[1,3,768]{2,0,1:T(1,128)}, u32[]{:S(2)}) copy-start(f32[1,3,768]{2,0,1:T(1,128)} %param.13) | copy-start | bytes 27652
  2.7 0.7 %copy-start.11 = (s32[768]{0:T(1024)S(1)}, s32[768]{0:T(1024)}, u32[]{:S(2)}) copy-start(s32[768]{0:T(1024)} %param.19) | copy-start | bytes 9220
  3.4 0.7 %copy-start.6 = (f32[1,3,768]{2,0,1:T(1,128)S(1)}, f32[1,3,768]{2,0,1:T(1,128)}, u32[]{:S(2)}) copy-start(f32[1,3,768]{2,0,1:T(1,128)} %param.14) | copy-start | bytes 27652
  4.1 0.7 %copy-start.2 = (s32[6,14]{1,0:T(8,128)S(1)}, s32[6,14]{1,0:T(8,128)}, u32[]{:S(2)}) copy-start(s32[6,14]{1,0:T(8,128)} %lists.1) | copy-start | bytes 1012
  4.1 0.7 %copy-start.3 = (s32[2,256]{1,0:T(2,128)S(1)}, s32[2,256]{1,0:T(2,128)}, u32[]{:S(2)}) copy-start(s32[2,256]{1,0:T(2,128)} %spots.1) | copy-start | bytes 6148
  4.1 0.7 %copy-start.4 = (s32[6]{0:T(128)S(1)}, s32[6]{0:T(128)}, u32[]{:S(2)}) copy-start(s32[6]{0:T(128)} %param.23) | copy-start | bytes 76
  4.8 1.1 %copy-start = (f32[10,128,128]{2,1,0:T(8,128)S(1)}, f32[10,128,128]{2,1,0:T(8,128)}, u32[]{:S(2)}) copy-start(f32[10,128,128]{2,1,0:T(8,128)} %obs.1) | copy-start | bytes 1966084
  5.9 1.1 %copy-start.1 = (f32[10,128,128]{2,1,0:T(8,128)S(1)}, f32[10,128,128]{2,1,0:T(8,128)}, u32[]{:S(2)}) copy-start(f32[10,128,128]{2,1,0:T(8,128)} %vrs.1) | copy-start | bytes 1966084

commit v2 on v1

--- a/solution.py
+++ b/solution.py
@@ -36,7 +36,22 @@
 
 def kernel(
     dims,
-    loc,
+    loc_at,
+    vel_at,
+    mass_at,
+    load_at,
+    strength_at,
+    sigma_at,
+    flag_at,
+    spots_at,
+    lists_at,
+    tally_at,
+    warm_at,
+    obs,
+    vrs,
+    pos_out,
+    vel_out,
+    dev_out,
     vel,
     mass_ref,
     load_ref,
@@ -47,11 +62,6 @@
     lists,
     tally,
     warm,
-    obs,
-    vrs,
-    pos_out,
-    vel_out,
-    dev_out,
     crd,
     zz,
     gxs,
@@ -129,19 +139,35 @@
 
     row0 = pl.multiple_of(x * (rows // 2) + zh * 8, 8)
     tile = pl.ds(row0, 8)
-    local_copies = [
-        pltpu.make_async_copy(src.at[:, tile, :], dst.at[pl.ds(HALO, thick)], loc_sem.at[i])
-        for i, (src, dst) in enumerate(((obs, obst), (vrs, vrst)))
-    ]
-    for c in local_copies:
+    fetched = {
+        "loc": (loc_at, crd.at[0]),
+        "flag": (flag_at, flag_ref.at[0]),
+        "strength": (strength_at, strength_ref.at[0]),
+        "load": (load_at, load_ref.at[0]),
+        "sigma": (sigma_at, sigma_ref.at[0]),
+        "spots": (spots_at, spots),
+        "lists": (lists_at, lists),
+        "tally": (tally_at, tally),
+        "obs": (obs.at[:, tile, :], obst.at[pl.ds(HALO, thick)]),
+        "vrs": (vrs.at[:, tile, :], vrst.at[pl.ds(HALO, thick)]),
+        "vel": (vel_at, vel),
+        "mass": (mass_at, mass_ref.at[0]),
+        "warm": (warm_at, warm),
+    }
+    copies = {
+        name: pltpu.make_async_copy(src, dst, loc_sem.at[i])
+        for i, (name, (src, dst)) in enumerate(fetched.items())
+    }
+    for c in copies.values():
         c.start()
+    for name in ("loc", "flag", "strength", "load", "sigma", "spots"):
+        copies[name].wait()
+    loc = crd.at[0]
     occ = flag_ref[...].astype(jnp.float32)
     amp = occ * strength_ref[...]
     q = occ * load_ref[...]
     sigma = sigma_ref[...]
     iv = 1.0 / (sigma * sigma)
-    for i in range(3):
-        crd[0, i] = loc[0, i : i + 1, :]
 
     sends = []
 
@@ -182,7 +208,7 @@
             )
         )
 
-    four = jnp.concatenate([loc[0], q], axis=0)
+    four = jnp.concatenate([loc[0], loc[1], loc[2], q], axis=0)
     first = four.astype(jnp.bfloat16).astype(jnp.float32)
     rest = four - first
     second = rest.astype(jnp.bfloat16).astype(jnp.float32)
@@ -234,7 +260,7 @@
     for c in range(cells):
         at = slice(c * CELL, (c + 1) * CELL)
         for i, col in enumerate((colx, coly, colz)):
-            v = jnp.broadcast_to(loc[0, i : i + 1, at], (CELL, CELL)).T
+            v = jnp.broadcast_to(loc[i, :, at], (CELL, CELL)).T
             col[at] = v * 2.0**shift_z if i == 0 else fixed(v, (rows, depth)[i - 1])
 
     for t, d in enumerate(near):
@@ -256,9 +282,9 @@
     scale_x = 2.0**shift_z
     for c in range(cells):
         at = slice(c * CELL, (c + 1) * CELL)
-        bx[c] = loc[0, 0:1, at] * scale_x
-        by[c] = fixed(loc[0, 1:2, at], rows)
-        bz[c] = fixed(loc[0, 2:3, at], depth)
+        bx[c] = loc[0, :, at] * scale_x
+        by[c] = fixed(loc[1, :, at], rows)
+        bz[c] = fixed(loc[2, :, at], depth)
         bq[c] = q[:, at]
     zero = jnp.zeros((1, CELL), jnp.float32)
     none = cells + 4
@@ -291,7 +317,7 @@
         xi, yi, zi = colx[at], coly[at], colz[at]
         total = [jnp.zeros((part_rows, CELL), jnp.float32)] * 3
         for s in range(slots):
-            n = jnp.where(s < tally[0, c], lists[c, s], none)
+            n = jnp.where(s < tally[c], lists[c, s], none)
             dx = xi - bx[n]
             dy = (yi - by[n]).astype(jnp.float32)
             dz = (zi - bz[n]).astype(jnp.float32)
@@ -305,10 +331,12 @@
         return 0
 
     units = cells * parts
+    copies["lists"].wait()
+    copies["tally"].wait()
     lax.fori_loop(0, units // 3, pair, 0)
 
-    for c in local_copies:
-        c.wait()
+    copies["obs"].wait()
+    copies["vrs"].wait()
     for c in ob_in + rs_in + lo_in + hi_in:
         c.wait_recv()
     total = acc[x] + rs[0] + rs[1] + rs[2]
@@ -368,6 +396,8 @@
 
     for c in fr_in:
         c.wait_recv()
+    for name in ("vel", "mass", "warm"):
+        copies[name].wait()
     mass = mass_ref[...]
     v_half = []
     square = jnp.zeros((1, atoms), jnp.float32)
@@ -375,7 +405,7 @@
         f = frc[0, i]
         for d in range(1, na):
             f = f + frcin[d, i]
-        v = vel[0, i : i + 1, :] + timestep * (short[i] - amp * f) / mass
+        v = vel[i] + timestep * (short[i] - amp * f) / mass
         square = square + mass * v * v
         v_half.append(v)
     row = square[:, :CELL]
@@ -392,12 +422,12 @@
         row = row + kin[d]
     kinetic = jnp.sum(row, axis=1, keepdims=True)
     present = kinetic / (3 * atoms * bricks * boltzmann) + 1e-06
-    wanted = jnp.full((1, 1), warm[0, 0].astype(jnp.float32))
+    wanted = jnp.full((1, 1), warm[0].astype(jnp.float32))
     ratio = jnp.sqrt(1.0 + heat_bath_damping * (wanted / present - 1.0))
     for i in range(3):
         v = ratio * v_half[i]
-        vel_out[0, i : i + 1, :] = v
-        pos_out[0, i : i + 1, :] = loc[0, i : i + 1, :] + timestep * v
+        vel_out[i] = v
+        pos_out[i] = loc[i] + timestep * v
     for c in sends:
         c.wait_send()
 
@@ -427,10 +457,19 @@
     blocks = cells + 5
     f32, bf16, i32 = jnp.float32, jnp.bfloat16, jnp.int32
     vmem = pl.BlockSpec(memory_space=pltpu.VMEM)
-    smem = pl.BlockSpec(memory_space=pltpu.SMEM)
-    anywhere = pl.BlockSpec(memory_space=pl.ANY)
+    hbm = pl.BlockSpec(memory_space=pltpu.HBM)
     edge = 2 * HALO * 8
     scratch = [
+        pltpu.VMEM((3, 1, atoms), f32),
+        pltpu.VMEM((1, atoms), f32),
+        pltpu.VMEM((1, atoms), f32),
+        pltpu.VMEM((1, atoms), f32),
+        pltpu.VMEM((1, atoms), f32),
+        pltpu.VMEM((1, atoms), i32),
+        pltpu.VMEM((2, GHOST), i32),
+        pltpu.SMEM(paired_partner_lists.shape, i32),
+        pltpu.SMEM((cells,), i32),
+        pltpu.SMEM((1,), i32),
         pltpu.VMEM((na, 3, 1, atoms), f32),
         pltpu.VMEM((na, depth, 2 * atoms), bf16),
         pltpu.VMEM((na, 16, atoms), f32),
@@ -458,19 +497,19 @@
         pltpu.VMEM((atoms, CELL), i32),
         pltpu.VMEM((3, atoms, CELL), f32),
         pltpu.VMEM((bricks, 1, CELL), f32),
-        pltpu.SemaphoreType.DMA((2,)),
+        pltpu.SemaphoreType.DMA((13,)),
     ]
     for count in (na, 2, 4, 4, 4, 4, 1, na, bricks):
         scratch += [pltpu.SemaphoreType.DMA((count,))] * 2
-    flat = lambda v: v.reshape(1, -1)
-    return pl.pallas_call(
+    tall = lambda v: v.reshape(3, 1, atoms)
+    new_positions, new_velocities, deviation = pl.pallas_call(
         functools.partial(kernel, (members, bricks, thick, rows, depth, atoms)),
         out_shape=(
-            jax.ShapeDtypeStruct((1, 3, atoms), f32),
-            jax.ShapeDtypeStruct((1, 3, atoms), f32),
+            jax.ShapeDtypeStruct((3, 1, atoms), f32),
+            jax.ShapeDtypeStruct((3, 1, atoms), f32),
             jax.ShapeDtypeStruct((thick, rows // members, depth), f32),
         ),
-        in_specs=[vmem] * 8 + [smem] * 3 + [anywhere] * 2,
+        in_specs=[hbm] * 13,
         out_specs=(vmem, vmem, vmem),
         scratch_shapes=scratch,
         compiler_params=pltpu.CompilerParams(
@@ -480,19 +519,29 @@
             flops=1_200_000_000, bytes_accessed=400_000, transcendentals=4_000_000
         ),
     )(
-        atom_locations,
-        atom_speeds_vector,
-        flat(inertial_amounts),
-        flat(electric_loads),
-        flat(scatter_strengths),
-        flat(gaussian_spreads_sigma),
-        flat(atom_present_flags),
-        halo_sender_spots,
-        paired_partner_lists,
-        flat(cell_usage_tally),
-        flat(target_warmth_levels),
-        observed_volume_values,
-        voxel_reciprocal_spread,
+        *(
+            pltpu.with_memory_space_constraint(v, pltpu.HBM)
+            for v in (
+                tall(atom_locations),
+                tall(atom_speeds_vector),
+                inertial_amounts,
+                electric_loads,
+                scatter_strengths,
+                gaussian_spreads_sigma,
+                atom_present_flags,
+                halo_sender_spots,
+                paired_partner_lists,
+                cell_usage_tally,
+            )
+        ),
+        target_warmth_levels,
+        pltpu.with_memory_space_constraint(observed_volume_values, pltpu.HBM),
+        pltpu.with_memory_space_constraint(voxel_reciprocal_spread, pltpu.HBM),
+    )
+    return (
+        new_positions.reshape(1, 3, atoms),
+        new_velocities.reshape(1, 3, atoms),
+        deviation,
     )
 
 

time: 55.8 us -> 49.4 us (0.89)
  local copies, waits for them, and re-layouts: 7.43 us -> 1.8 us
    unnamed x27 -> x3, local copies, waits for them, and re-layouts: 6.2 us -> 1.8 us
    pallas_call x2 -> x0, local copies, waits for them, and re-layouts: 1.22 us -> none  [local(): pl.pallas_call(functools.partial(kernel, (members, bricks, thick, rows, d...]
where the time goes in v2:
time: 49.4 us; the launch traced here: 49.3 us
  Pallas kernels  46.2 us (94%)
  local copies, waits for them, and re-layouts  1.8 us (4%)
  between operations  1.29 us (3%)
    pallas_call x1, Pallas kernels, local(): pl.pallas_call(functools.partial(kernel, (members, bricks, thick, rows, d...  46.2 us
    unnamed x3, local copies, waits for them, and re-layouts  1.8 us

profile of v2, /device:TPU:1, one launch (start us, length us, event | category | flops | bytes accessed | tf_op | source)
XLA Modules:
  0.0 49.3 jit_solution(5387204562108634518)
XLA Ops:
  1.3 46.2 %shard_map.148 = (f32[3,1,768]{2,1,0:T(1,128)S(1)}, f32[3,1,768]{2,1,0:T(1,128)S(1)}, f32[10,4,128]{2,1,0:T(4,128)S(1)}) custom-call(f32[3,1,768]{2,1,0:T(1,128)} %bitcast.6, f32[3,1,768]{2,1,0:T(1,128)} %bitcast.7, f32[768]{0:T(1024)} %mass_at.1, f32[768]{0:T(1024)} %load_at.1, f32[768]{0:T(1024)} %strength_at.1, f32[768]{0:T(1024)} %sigma_at.1, ...), custom_call_target="tpu_custom_call" | custom-call | flops 1200000000 | bytes 400000 | tf_op jit(solution)/shard_map/pallas_call | solution.py:505
  47.4 0.6 %copy.20 = f32[1,3,768]{2,0,1:T(1,128)} copy(f32[1,3,768]{2,0,1:T(1,128)S(1)} %bitcast.5) | data formatting | bytes 18432
  48.0 0.6 %copy.21 = f32[1,3,768]{2,0,1:T(1,128)} copy(f32[1,3,768]{2,0,1:T(1,128)S(1)} %bitcast.4) | data formatting | bytes 18432
  48.6 0.6 %copy.22 = f32[10,4,128]{2,1,0:T(4,128)} copy(f32[10,4,128]{2,1,0:T(4,128)S(1)} %get-tuple-element.14) | data formatting | bytes 40960

commit v3 on v2

--- a/solution.py
+++ b/solution.py
@@ -21,8 +21,6 @@
 timestep = 0.5
 boltzmann = 0.015
 heat_bath_damping = 0.5
-
-B_STEPS = ((0, 0), (0, 1), (1, 0), (1, 1))
 
 
 def fixed(coord, period):
@@ -72,8 +70,9 @@
     rs,
     lo,
     hi,
-    obst,
-    vrst,
+    obv,
+    amps,
+    ivs,
     grd,
     frc,
     frcin,
@@ -102,43 +101,39 @@
     lo_rs,
     hi_ss,
     hi_rs,
-    gr_ss,
-    gr_rs,
     fr_ss,
     fr_rs,
     kn_ss,
     kn_rs,
 ):
     members, bricks, thick, rows, depth, atoms = dims
-    half = members // 2
-    na = half // 2
+    na = members // 2
+    share = rows // members
     planes = thick + 2 * HALO
     wide = planes * 8
+    edge = 2 * HALO * 8
     cells = atoms // CELL
     slots = lists.shape[1]
     r = lax.axis_index("replica")
     b = lax.axis_index("brick")
-    x, z = r // half, r % half
-    zh, zp = z // 2, z % 2
+    x, z = r // na, r % na
     up, down = (b + 1) % bricks, (b + bricks - 1) % bricks
+    across = ((1 - x) * na + z, b)
 
     def a_peer(d):
-        return (x * half + ((zh + d) % na) * 2 + zp, b)
-
-    def b_rep(k):
-        dx, dp = B_STEPS[k]
-        return ((x + dx) % 2) * half + zh * 2 + (zp + dp) % 2
+        return (x * na + (z + d) % na, b)
+
+    def nearest(t):
+        odd = t % 2
+        return odd * ((t + 1) // 2) + (1 - odd) * ((na - t // 2) % na)
 
     barrier = pltpu.get_barrier_semaphore()
-    partners = [a_peer(d) for d in range(1, na)]
-    partners += [(b_rep(k), b) for k in range(1, 4)]
-    partners += [(b_rep(k), n) for k in range(1, 4) for n in (up, down)]
+    partners = [a_peer(d) for d in range(1, na)] + [across]
+    partners += [(across[0], up), (across[0], down)]
     partners += [(r, (b + d) % bricks) for d in range(1, bricks)]
     for p in partners:
         pl.semaphore_signal(barrier, inc=1, device_id=p, device_id_type=MESH)
 
-    row0 = pl.multiple_of(x * (rows // 2) + zh * 8, 8)
-    tile = pl.ds(row0, 8)
     fetched = {
         "loc": (loc_at, crd.at[0]),
         "flag": (flag_at, flag_ref.at[0]),
@@ -148,12 +143,14 @@
         "spots": (spots_at, spots),
         "lists": (lists_at, lists),
         "tally": (tally_at, tally),
-        "obs": (obs.at[:, tile, :], obst.at[pl.ds(HALO, thick)]),
-        "vrs": (vrs.at[:, tile, :], vrst.at[pl.ds(HALO, thick)]),
         "vel": (vel_at, vel),
         "mass": (mass_at, mass_ref.at[0]),
         "warm": (warm_at, warm),
     }
+    for t in range(2):
+        tile = pl.ds(pl.multiple_of(t * (rows // 2) + (z // 2) * 8, 8), 8)
+        for i, src in enumerate((obs, vrs)):
+            fetched["map", t, i] = (src.at[:, tile, :], obv.at[pl.ds(HALO, thick), i, t])
     copies = {
         name: pltpu.make_async_copy(src, dst, loc_sem.at[i])
         for i, (name, (src, dst)) in enumerate(fetched.items())
@@ -169,45 +166,6 @@
     sigma = sigma_ref[...]
     iv = 1.0 / (sigma * sigma)
 
-    sends = []
-
-    def remote(src, dst, ss, rsem, device):
-        c = pltpu.make_async_remote_copy(
-            src_ref=src, dst_ref=dst, send_sem=ss, recv_sem=rsem, device_id=device, device_id_type=MESH
-        )
-        c.start()
-        sends.append(c)
-        return c
-
-    near = []
-    for t in range(1, na):
-        near.append((t + 1) // 2 if t % 2 else na - t // 2)
-
-    pl.semaphore_wait(barrier, len(partners))
-    crd_in = {}
-    for d in reversed(near):
-        crd_in[d] = remote(crd.at[0], crd.at[d], crd_ss.at[d], crd_rs.at[d], a_peer(d))
-    ob_in = []
-    for i, (src, dst) in enumerate(((obs, obst), (vrs, vrst))):
-        ob_in.append(
-            remote(
-                src.at[pl.ds(thick - HALO, HALO), tile, :],
-                dst.at[pl.ds(0, HALO)],
-                ob_ss.at[2 * i],
-                ob_rs.at[2 * i],
-                (r, up),
-            )
-        )
-        ob_in.append(
-            remote(
-                src.at[pl.ds(0, HALO), tile, :],
-                dst.at[pl.ds(thick + HALO, HALO)],
-                ob_ss.at[2 * i + 1],
-                ob_rs.at[2 * i + 1],
-                (r, down),
-            )
-        )
-
     four = jnp.concatenate([loc[0], loc[1], loc[2], q], axis=0)
     first = four.astype(jnp.bfloat16).astype(jnp.float32)
     rest = four - first
@@ -215,23 +173,24 @@
     third = rest - second
     pieces = jnp.concatenate([first, second, third, jnp.zeros_like(four)], axis=0).astype(jnp.bfloat16)
     slot_of = lax.broadcasted_iota(jnp.int32, (atoms, GHOST), 0)
-    gh_in = []
-    for side, (dst, device) in enumerate(((glo, (r, up)), (ghi, (r, down)))):
+    for side in range(2):
         chosen = jnp.where(slot_of == spots[side : side + 1, :], 1.0, 0.0).astype(jnp.bfloat16)
         got = jnp.dot(pieces, chosen, preferred_element_type=jnp.float32)
         got = got[0:4] + got[4:8] + got[8:12]
         for i in range(4):
             gsend[side, i] = got[i : i + 1]
-        gh_in.append(remote(gsend.at[side], dst, gh_ss.at[side], gh_rs.at[side], device))
 
     shift_y, shift_z = 32 - int(math.log2(rows)), 32 - int(math.log2(depth))
     unit_y, unit_z = 2.0**-shift_y, 2.0**-shift_z
-    ivc = iv * (-0.5 * LOG2E)
-    plane_at = (b * thick - HALO + lax.broadcasted_iota(jnp.int32, (16, atoms), 0)).astype(jnp.float32)
-    row_in = lax.broadcasted_iota(jnp.int32, (16, atoms), 0)
-    row_at = (zh * 8 + (row_in // 8) * (rows // 2) + row_in % 8) << shift_y
-
-    def spread(d, start):
+    amps[...] = amp
+    ivs[...] = iv
+
+    def spread(d):
+        amp, iv = amps[...], ivs[...]
+        ivc = iv * (-0.5 * LOG2E)
+        plane_at = (b * thick - HALO + lax.broadcasted_iota(jnp.int32, (16, atoms), 0)).astype(jnp.float32)
+        row_in = lax.broadcasted_iota(jnp.int32, (8, atoms), 0)
+        row_at = (z * share + (row_in // share) * (rows // 2) + row_in % share) << shift_y
         dx = plane_at - crd[d, 0]
         gx = jnp.exp2(dx * dx * ivc)
         gxs[d] = gx
@@ -246,38 +205,16 @@
         zz[d, :, atoms:] = (dz * (iv * unit_z) * gz).astype(jnp.bfloat16)
         gzb = gz.astype(jnp.bfloat16)
         zz[d, :, :atoms] = gzb
-        ax = (amp * gx)[:planes]
-        for t in range(2):
-            left = ax[:, None, :] * gy[None, 8 * t : 8 * t + 8, :]
-            part = dot_t(left.reshape(wide, atoms).astype(jnp.bfloat16), gzb)
-            if start:
-                acc[t] = part
-            else:
-                acc[t] += part
-
-    spread(0, True)
+        left = (amp * gx)[:planes, None, :] * gy[None]
+        acc[...] += dot_t(left.reshape(wide, atoms).astype(jnp.bfloat16), gzb)
+
+    acc[...] = jnp.zeros_like(acc)
 
     for c in range(cells):
         at = slice(c * CELL, (c + 1) * CELL)
         for i, col in enumerate((colx, coly, colz)):
             v = jnp.broadcast_to(loc[i, :, at], (CELL, CELL)).T
             col[at] = v * 2.0**shift_z if i == 0 else fixed(v, (rows, depth)[i - 1])
-
-    for t, d in enumerate(near):
-        crd_in[d].wait_recv()
-        spread(d, False)
-
-    rs_in, lo_in, hi_in = [], [], []
-    edge = 2 * HALO * 8
-    for k in (3, 2, 1, 0):
-        dx, dp = B_STEPS[k]
-        t = (x + dx) % 2
-        if k:
-            rs_in.append(remote(acc.at[t], rs.at[k - 1], rs_ss.at[k], rs_rs.at[k], (b_rep(k), b)))
-        lo_in.append(
-            remote(acc.at[t, pl.ds(wide - edge, edge)], lo.at[k], lo_ss.at[k], lo_rs.at[k], (b_rep(k), up))
-        )
-        hi_in.append(remote(acc.at[t, pl.ds(0, edge)], hi.at[k], hi_ss.at[k], hi_rs.at[k], (b_rep(k), down)))
 
     scale_x = 2.0**shift_z
     for c in range(cells):
@@ -286,12 +223,68 @@
         by[c] = fixed(loc[1, :, at], rows)
         bz[c] = fixed(loc[2, :, at], depth)
         bq[c] = q[:, at]
-    zero = jnp.zeros((1, CELL), jnp.float32)
     none = cells + 4
-    bx[none] = zero
-    bq[none] = zero
-    by[none] = jnp.zeros((1, CELL), jnp.int32)
-    bz[none] = jnp.zeros((1, CELL), jnp.int32)
+    for ref in (bx, bq, by, bz):
+        ref[none] = jnp.zeros((1, CELL), ref.dtype)
+
+    sends = []
+
+    def remote(src, dst, ss, rsem, device):
+        return pltpu.make_async_remote_copy(
+            src_ref=src, dst_ref=dst, send_sem=ss, recv_sem=rsem, device_id=device, device_id_type=MESH
+        )
+
+    def post(*a):
+        c = remote(*a)
+        c.start()
+        sends.append(c)
+        return c
+
+    def crd_copy(d):
+        return remote(crd.at[0], crd.at[d], crd_ss.at[d], crd_rs.at[d], a_peer(d))
+
+    pl.semaphore_wait(barrier, len(partners))
+    for t in range(na - 1, 0, -1):
+        crd_copy(nearest(t)).start()
+    gh_in = [
+        post(gsend.at[0], glo, gh_ss.at[0], gh_rs.at[0], (r, up)),
+        post(gsend.at[1], ghi, gh_ss.at[1], gh_rs.at[1], (r, down)),
+    ]
+    for t in range(2):
+        for i in range(2):
+            copies["map", t, i].wait()
+    ob_in = [
+        post(obv.at[pl.ds(thick, HALO)], obv.at[pl.ds(0, HALO)], ob_ss.at[0], ob_rs.at[0], (r, up)),
+        post(
+            obv.at[pl.ds(HALO, HALO)],
+            obv.at[pl.ds(thick + HALO, HALO)],
+            ob_ss.at[1],
+            ob_rs.at[1],
+            (r, down),
+        ),
+    ]
+
+    def collect(t, _):
+        d = nearest(t)
+
+        @pl.when(t > 0)
+        def _():
+            crd_copy(d).wait_recv()
+
+        spread(d)
+        return 0
+
+    lax.fori_loop(0, na, collect, 0)
+
+    lower, upper = acc.at[pl.ds(0, edge)], acc.at[pl.ds(wide - edge, edge)]
+    map_in = [
+        post(upper, lo.at[0], lo_ss.at[0], lo_rs.at[0], (across[0], up)),
+        post(lower, hi.at[0], hi_ss.at[0], hi_rs.at[0], (across[0], down)),
+        post(upper, lo.at[1], lo_ss.at[1], lo_rs.at[1], (r, up)),
+        post(lower, hi.at[1], hi_ss.at[1], hi_rs.at[1], (r, down)),
+        post(acc, rs, rs_ss.at[0], rs_rs.at[0], across),
+    ]
+
     for c in gh_in:
         c.wait_recv()
     period_x = float(thick * bricks)
@@ -333,27 +326,30 @@
     units = cells * parts
     copies["lists"].wait()
     copies["tally"].wait()
-    lax.fori_loop(0, units // 3, pair, 0)
-
-    copies["obs"].wait()
-    copies["vrs"].wait()
-    for c in ob_in + rs_in + lo_in + hi_in:
+    lax.fori_loop(0, units // 2, pair, 0)
+
+    for c in ob_in + map_in:
         c.wait_recv()
-    total = acc[x] + rs[0] + rs[1] + rs[2]
-    low = lo[0] + lo[1] + lo[2] + lo[3]
-    high = hi[0] + hi[1] + hi[2] + hi[3]
+    total = acc[...] + rs[...]
+    low = lo[0] + lo[1]
+    high = hi[0] + hi[1]
     total = jnp.concatenate(
         [total[:edge] + low, total[edge : wide - edge], total[wide - edge :] + high], axis=0
-    )
-    dev = total.reshape(planes, 8, depth) / members - obst[...]
-    grad = (restraint * vrst[...] * dev).astype(jnp.bfloat16)
-    grd[x] = grad.reshape(wide, depth)
-    gr_in = remote(grd.at[x], grd.at[x], gr_ss.at[0], gr_rs.at[0], (b_rep(2), b))
+    ).reshape(planes, 8, depth)
+    row_in = lax.broadcasted_iota(jnp.int32, (planes, 8, depth), 1)
+
+    def own_rows(i):
+        one, two = obv[:, i, 0], obv[:, i, 1]
+        turn = lambda v: jnp.concatenate([v[:, share:], v[:, :share]], axis=1)
+        even = jnp.where(row_in < share, one, turn(two))
+        odd = jnp.where(row_in < share, turn(one), two)
+        return jnp.where(z % 2 == 0, even, odd)
+
+    dev = total / members - own_rows(0)
+    grad = (restraint * own_rows(1) * dev).astype(jnp.bfloat16)
+    grd[...] = grad.reshape(wide, depth)
     own = dev[HALO : HALO + thick]
-    dev_out[...] = jnp.where(zp == 0, own[:, :4], own[:, 4:])
-
-    lax.fori_loop(units // 3, 2 * units // 3, pair, 0)
-    gr_in.wait_recv()
+    dev_out[...] = jnp.where(x == 0, own[:, :share], own[:, share:])
 
     lanes = 256
 
@@ -361,60 +357,65 @@
         for c in range(atoms // lanes):
             at = slice(c * lanes, (c + 1) * lanes)
             after = slice(atoms + c * lanes, atoms + (c + 1) * lanes)
-            f = [0.0, 0.0, 0.0]
-            for t in range(2):
-                along = jnp.dot(grd[t], zz[d, :, at], preferred_element_type=jnp.float32)
-                across = jnp.dot(grd[t], zz[d, :, after], preferred_element_type=jnp.float32)
-                sums = [0.0, 0.0, 0.0]
-                for i in range(planes):
-                    p = along[8 * i : 8 * i + 8]
-                    g = gxs[d, i : i + 1, at]
-                    sums[0] += gxds[d, i : i + 1, at] * p
-                    sums[1] += g * p
-                    sums[2] += g * across[8 * i : 8 * i + 8]
-                y = gys[d, 8 * t : 8 * t + 8, at]
-                f[0] += y * sums[0]
-                f[1] += gyds[d, 8 * t : 8 * t + 8, at] * sums[1]
-                f[2] += y * sums[2]
+            along = jnp.dot(grd[...], zz[d, :, at], preferred_element_type=jnp.float32)
+            slope = jnp.dot(grd[...], zz[d, :, after], preferred_element_type=jnp.float32)
+            sums = [0.0, 0.0, 0.0]
+            for i in range(planes):
+                p = along[8 * i : 8 * i + 8]
+                g = gxs[d, i : i + 1, at]
+                sums[0] += gxds[d, i : i + 1, at] * p
+                sums[1] += g * p
+                sums[2] += g * slope[8 * i : 8 * i + 8]
+            y = gys[d, :, at]
+            f = (y * sums[0], gyds[d, :, at] * sums[1], y * sums[2])
             for i in range(3):
                 frc[d, i, :, at] = jnp.sum(f[i], axis=0, keepdims=True)
 
-    fr_in = []
-    for d in reversed(near):
+    def fr_copy(d):
+        return remote(frc.at[d], frcin.at[d], fr_ss.at[d], fr_rs.at[d], a_peer((na - d) % na))
+
+    def give(t, _):
+        d = nearest(na - 1 - t)
         force(d)
-        fr_in.append(remote(frc.at[d], frcin.at[d], fr_ss.at[d], fr_rs.at[d], a_peer(na - d)))
-    force(0)
-
-    lax.fori_loop(2 * units // 3, units, pair, 0)
-    short = []
-    gain = coupling * 4.0**shift_z
+
+        @pl.when(t < na - 1)
+        def _():
+            fr_copy(d).start()
+
+        return 0
+
+    lax.fori_loop(0, na, give, 0)
+
+    lax.fori_loop(units // 2, units, pair, 0)
+    for name in ("vel", "mass", "warm"):
+        copies[name].wait()
+    mass = mass_ref[...]
+    light = timestep / mass
+    gain = (coupling * 4.0**shift_z) * q * light
+    push = amps[...] * light
+    v_half = []
     for i in range(3):
         line = [
             jnp.sum(pacc[i, c * CELL : (c + 1) * CELL].T, axis=0, keepdims=True) for c in range(cells)
         ]
-        short.append((gain * q) * jnp.concatenate(line, axis=1))
-
-    for c in fr_in:
-        c.wait_recv()
-    for name in ("vel", "mass", "warm"):
-        copies[name].wait()
-    mass = mass_ref[...]
-    v_half = []
+        v_half.append(vel[i] + gain * jnp.concatenate(line, axis=1))
+
+    for d in range(1, na):
+        fr_copy(d).wait_recv()
     square = jnp.zeros((1, atoms), jnp.float32)
     for i in range(3):
         f = frc[0, i]
         for d in range(1, na):
             f = f + frcin[d, i]
-        v = vel[i] + timestep * (short[i] - amp * f) / mass
-        square = square + mass * v * v
-        v_half.append(v)
+        v_half[i] = v_half[i] - push * f
+        square = square + v_half[i] * v_half[i]
+    square = mass * square
     row = square[:, :CELL]
     for c in range(1, cells):
         row = row + square[:, c * CELL : (c + 1) * CELL]
     kin[0] = row
     kn_in = [
-        remote(kin.at[0], kin.at[d], kn_ss.at[d], kn_rs.at[d], (r, (b + d) % bricks))
-        for d in range(1, bricks)
+        post(kin.at[0], kin.at[d], kn_ss.at[d], kn_rs.at[d], (r, (b + d) % bricks)) for d in range(1, bricks)
     ]
     for c in kn_in:
         c.wait_recv()
@@ -428,6 +429,9 @@
         v = ratio * v_half[i]
         vel_out[i] = v
         pos_out[i] = loc[i] + timestep * v
+    for d in range(1, na):
+        crd_copy(d).wait_send()
+        fr_copy(d).wait_send()
     for c in sends:
         c.wait_send()
 
@@ -450,7 +454,7 @@
     thick, rows, depth = observed_volume_values.shape
     atoms = atom_locations.shape[2]
     members, bricks = lax.axis_size("replica"), lax.axis_size("brick")
-    na = members // 4
+    na = members // 2
     planes = thick + 2 * HALO
     wide = planes * 8
     cells = atoms // CELL
@@ -474,15 +478,16 @@
         pltpu.VMEM((na, depth, 2 * atoms), bf16),
         pltpu.VMEM((na, 16, atoms), f32),
         pltpu.VMEM((na, 16, atoms), f32),
-        pltpu.VMEM((na, 16, atoms), f32),
-        pltpu.VMEM((na, 16, atoms), f32),
-        pltpu.VMEM((2, wide, depth), f32),
-        pltpu.VMEM((3, wide, depth), f32),
-        pltpu.VMEM((4, edge, depth), f32),
-        pltpu.VMEM((4, edge, depth), f32),
-        pltpu.VMEM((planes, 8, depth), f32),
-        pltpu.VMEM((planes, 8, depth), f32),
-        pltpu.VMEM((2, wide, depth), bf16),
+        pltpu.VMEM((na, 8, atoms), f32),
+        pltpu.VMEM((na, 8, atoms), f32),
+        pltpu.VMEM((wide, depth), f32),
+        pltpu.VMEM((wide, depth), f32),
+        pltpu.VMEM((2, edge, depth), f32),
+        pltpu.VMEM((2, edge, depth), f32),
+        pltpu.VMEM((planes, 2, 2, 8, depth), f32),
+        pltpu.VMEM((1, atoms), f32),
+        pltpu.VMEM((1, atoms), f32),
+        pltpu.VMEM((wide, depth), bf16),
         pltpu.VMEM((na, 3, 1, atoms), f32),
         pltpu.VMEM((na, 3, 1, atoms), f32),
         pltpu.VMEM((2, 4, 1, GHOST), f32),
@@ -497,9 +502,9 @@
         pltpu.VMEM((atoms, CELL), i32),
         pltpu.VMEM((3, atoms, CELL), f32),
         pltpu.VMEM((bricks, 1, CELL), f32),
-        pltpu.SemaphoreType.DMA((13,)),
+        pltpu.SemaphoreType.DMA((15,)),
     ]
-    for count in (na, 2, 4, 4, 4, 4, 1, na, bricks):
+    for count in (na, 2, 2, 1, 2, 2, na, bricks):
         scratch += [pltpu.SemaphoreType.DMA((count,))] * 2
     tall = lambda v: v.reshape(3, 1, atoms)
     new_positions, new_velocities, deviation = pl.pallas_call(

time: 49.4 us -> 53.2 us (1.077)
  Pallas kernels: 46.2 us -> 49.9 us
    pallas_call x1, Pallas kernels: 46.2 us -> 49.9 us  [local(): pl.pallas_call(functools.partial(kernel, (members, bricks, thick, rows, d...]
where the time goes in v3:
time: 53.2 us; the launch traced here: 53 us
  Pallas kernels  49.9 us (94%)
  local copies, waits for them, and re-layouts  1.8 us (3%)
  between operations  1.29 us (2%)
    pallas_call x1, Pallas kernels, local(): pl.pallas_call(functools.partial(kernel, (members, bricks, thick, rows, d...  49.9 us
    unnamed x3, local copies, waits for them, and re-layouts  1.8 us

profile of v3, /device:TPU:1, one launch (start us, length us, event | category | flops | bytes accessed | tf_op | source)
XLA Modules:
  0.0 53.0 jit_solution(2714406886814140145)
XLA Ops:
  1.3 49.9 %shard_map.148 = (f32[3,1,768]{2,1,0:T(1,128)S(1)}, f32[3,1,768]{2,1,0:T(1,128)S(1)}, f32[10,4,128]{2,1,0:T(4,128)S(1)}) custom-call(f32[3,1,768]{2,1,0:T(1,128)} %bitcast.6, f32[3,1,768]{2,1,0:T(1,128)} %bitcast.7, f32[768]{0:T(1024)} %mass_at.1, f32[768]{0:T(1024)} %load_at.1, f32[768]{0:T(1024)} %strength_at.1, f32[768]{0:T(1024)} %sigma_at.1, ...), custom_call_target="tpu_custom_call" | custom-call | flops 1200000000 | bytes 400000 | tf_op jit(solution)/shard_map/pallas_call | solution.py:510
  51.2 0.6 %copy.20 = f32[1,3,768]{2,0,1:T(1,128)} copy(f32[1,3,768]{2,0,1:T(1,128)S(1)} %bitcast.5) | data formatting | bytes 18432
  51.8 0.6 %copy.21 = f32[1,3,768]{2,0,1:T(1,128)} copy(f32[1,3,768]{2,0,1:T(1,128)S(1)} %bitcast.4) | data formatting | bytes 18432
  52.4 0.6 %copy.22 = f32[10,4,128]{2,1,0:T(4,128)} copy(f32[10,4,128]{2,1,0:T(4,128)S(1)} %get-tuple-element.14) | data formatting | bytes 40960

commit v4 on v3

--- a/solution.py
+++ b/solution.py
@@ -14,6 +14,7 @@
 CELL = 128
 GHOST = 256
 LOG2E = 1.4426950408889634
+B_STEPS = ((0, 0), (0, 1), (1, 0), (1, 1))
 
 restraint = 0.1
 coupling = 5.0
@@ -67,6 +68,7 @@
     gys,
     gyds,
     acc,
+    mine,
     rs,
     lo,
     hi,
@@ -107,29 +109,40 @@
     kn_rs,
 ):
     members, bricks, thick, rows, depth, atoms = dims
-    na = members // 2
+    half = members // 2
+    na = half // 2
     share = rows // members
     planes = thick + 2 * HALO
-    wide = planes * 8
-    edge = 2 * HALO * 8
+    wide = planes * 16
+    edge = 2 * HALO * 16
     cells = atoms // CELL
     slots = lists.shape[1]
     r = lax.axis_index("replica")
     b = lax.axis_index("brick")
-    x, z = r // na, r % na
+    x, z = r // half, r % half
+    zh, zp = z // 2, z % 2
     up, down = (b + 1) % bricks, (b + bricks - 1) % bricks
-    across = ((1 - x) * na + z, b)
 
     def a_peer(d):
-        return (x * na + (z + d) % na, b)
+        return (x * half + ((zh + d) % na) * 2 + zp, b)
+
+    def b_rep(k):
+        dx, dp = B_STEPS[k]
+        return ((x + dx) % 2) * half + zh * 2 + (zp + dp) % 2
 
     def nearest(t):
         odd = t % 2
         return odd * ((t + 1) // 2) + (1 - odd) * ((na - t // 2) % na)
 
+    direct = [nearest(t) for t in range(1, na)]
+    relayed = {}
+    if na == 8:
+        direct = direct[:4]
+        relayed = {1: (3, 2), 7: (5, 6), 2: (4, 2)}
+
     barrier = pltpu.get_barrier_semaphore()
-    partners = [a_peer(d) for d in range(1, na)] + [across]
-    partners += [(across[0], up), (across[0], down)]
+    partners = [a_peer(d) for d in direct]
+    partners += [(b_rep(k), n) for k in range(1, 4) for n in (b, up, down)]
     partners += [(r, (b + d) % bricks) for d in range(1, bricks)]
     for p in partners:
         pl.semaphore_signal(barrier, inc=1, device_id=p, device_id_type=MESH)
@@ -148,9 +161,9 @@
         "warm": (warm_at, warm),
     }
     for t in range(2):
-        tile = pl.ds(pl.multiple_of(t * (rows // 2) + (z // 2) * 8, 8), 8)
+        tile = pl.ds(pl.multiple_of(t * (rows // 2) + zh * 8, 8), 8)
         for i, src in enumerate((obs, vrs)):
-            fetched["map", t, i] = (src.at[:, tile, :], obv.at[pl.ds(HALO, thick), i, t])
+            fetched["map", t, i] = (src.at[:, tile, :], obv.at[pl.ds(HALO, thick), i, pl.ds(8 * t, 8)])
     copies = {
         name: pltpu.make_async_copy(src, dst, loc_sem.at[i])
         for i, (name, (src, dst)) in enumerate(fetched.items())
@@ -189,8 +202,8 @@
         amp, iv = amps[...], ivs[...]
         ivc = iv * (-0.5 * LOG2E)
         plane_at = (b * thick - HALO + lax.broadcasted_iota(jnp.int32, (16, atoms), 0)).astype(jnp.float32)
-        row_in = lax.broadcasted_iota(jnp.int32, (8, atoms), 0)
-        row_at = (z * share + (row_in // share) * (rows // 2) + row_in % share) << shift_y
+        row_in = lax.broadcasted_iota(jnp.int32, (16, atoms), 0)
+        row_at = (zh * 8 + (row_in // 8) * (rows // 2) + row_in % 8) << shift_y
         dx = plane_at - crd[d, 0]
         gx = jnp.exp2(dx * dx * ivc)
         gxs[d] = gx
@@ -206,9 +219,13 @@
         gzb = gz.astype(jnp.bfloat16)
         zz[d, :, :atoms] = gzb
         left = (amp * gx)[:planes, None, :] * gy[None]
-        acc[...] += dot_t(left.reshape(wide, atoms).astype(jnp.bfloat16), gzb)
-
-    acc[...] = jnp.zeros_like(acc)
+        part = dot_t(left.reshape(wide, atoms).astype(jnp.bfloat16), gzb)
+        if d == 0:
+            acc[...] = part
+        else:
+            acc[...] += part
+
+    spread(0)
 
     for c in range(cells):
         at = slice(c * CELL, (c + 1) * CELL)
@@ -240,12 +257,10 @@
         sends.append(c)
         return c
 
-    def crd_copy(d):
-        return remote(crd.at[0], crd.at[d], crd_ss.at[d], crd_rs.at[d], a_peer(d))
-
     pl.semaphore_wait(barrier, len(partners))
-    for t in range(na - 1, 0, -1):
-        crd_copy(nearest(t)).start()
+    crd_in = {}
+    for d in reversed(direct):
+        crd_in[d] = post(crd.at[0], crd.at[d], crd_ss.at[d], crd_rs.at[d], a_peer(d))
     gh_in = [
         post(gsend.at[0], glo, gh_ss.at[0], gh_rs.at[0], (r, up)),
         post(gsend.at[1], ghi, gh_ss.at[1], gh_rs.at[1], (r, down)),
@@ -264,26 +279,31 @@
         ),
     ]
 
-    def collect(t, _):
-        d = nearest(t)
-
-        @pl.when(t > 0)
-        def _():
-            crd_copy(d).wait_recv()
-
-        spread(d)
-        return 0
-
-    lax.fori_loop(0, na, collect, 0)
-
-    lower, upper = acc.at[pl.ds(0, edge)], acc.at[pl.ds(wide - edge, edge)]
-    map_in = [
-        post(upper, lo.at[0], lo_ss.at[0], lo_rs.at[0], (across[0], up)),
-        post(lower, hi.at[0], hi_ss.at[0], hi_rs.at[0], (across[0], down)),
-        post(upper, lo.at[1], lo_ss.at[1], lo_rs.at[1], (r, up)),
-        post(lower, hi.at[1], hi_ss.at[1], hi_rs.at[1], (r, down)),
-        post(acc, rs, rs_ss.at[0], rs_rs.at[0], across),
-    ]
+    def await_crd(d):
+        crd_in[d].wait_recv()
+        if d in relayed:
+            far, to = relayed[d]
+            crd_in[far] = post(crd.at[d], crd.at[far], crd_ss.at[far], crd_rs.at[far], a_peer(to))
+
+    if na == 8:
+        for ready, then in (((1, 7), (1,)), ((2,), (7, 2)), ((6,), (6,)), ((3,), (3,)), ((5,), (5,)), ((4,), (4,))):
+            for d in ready:
+                await_crd(d)
+            for d in then:
+                spread(d)
+    else:
+        for d in direct:
+            await_crd(d)
+            spread(d)
+
+    mine[...] = acc[...].astype(jnp.bfloat16)
+    lower, upper = mine.at[pl.ds(0, edge)], mine.at[pl.ds(wide - edge, edge)]
+    map_in = []
+    for k in (3, 2, 1, 0):
+        map_in.append(post(upper, lo.at[k], lo_ss.at[k], lo_rs.at[k], (b_rep(k), up)))
+        map_in.append(post(lower, hi.at[k], hi_ss.at[k], hi_rs.at[k], (b_rep(k), down)))
+        if k:
+            map_in.append(post(mine, rs.at[k - 1], rs_ss.at[k], rs_rs.at[k], (b_rep(k), b)))
 
     for c in gh_in:
         c.wait_recv()
@@ -330,26 +350,19 @@
 
     for c in ob_in + map_in:
         c.wait_recv()
-    total = acc[...] + rs[...]
-    low = lo[0] + lo[1]
-    high = hi[0] + hi[1]
+    wider = lambda v: v.astype(jnp.float32)
+    total = acc[...] + wider(rs[0]) + wider(rs[1]) + wider(rs[2])
+    low = wider(lo[0]) + wider(lo[1]) + wider(lo[2]) + wider(lo[3])
+    high = wider(hi[0]) + wider(hi[1]) + wider(hi[2]) + wider(hi[3])
     total = jnp.concatenate(
         [total[:edge] + low, total[edge : wide - edge], total[wide - edge :] + high], axis=0
-    ).reshape(planes, 8, depth)
-    row_in = lax.broadcasted_iota(jnp.int32, (planes, 8, depth), 1)
-
-    def own_rows(i):
-        one, two = obv[:, i, 0], obv[:, i, 1]
-        turn = lambda v: jnp.concatenate([v[:, share:], v[:, :share]], axis=1)
-        even = jnp.where(row_in < share, one, turn(two))
-        odd = jnp.where(row_in < share, turn(one), two)
-        return jnp.where(z % 2 == 0, even, odd)
-
-    dev = total / members - own_rows(0)
-    grad = (restraint * own_rows(1) * dev).astype(jnp.bfloat16)
+    ).reshape(planes, 16, depth)
+    dev = total / members - obv[:, 0]
+    grad = (restraint * obv[:, 1] * dev).astype(jnp.bfloat16)
     grd[...] = grad.reshape(wide, depth)
     own = dev[HALO : HALO + thick]
-    dev_out[...] = jnp.where(x == 0, own[:, :share], own[:, share:])
+    own = jnp.where(x == 0, own[:, :8], own[:, 8:])
+    dev_out[...] = jnp.where(zp == 0, own[:, :share], own[:, share:])
 
     lanes = 256
 
@@ -361,11 +374,11 @@
             slope = jnp.dot(grd[...], zz[d, :, after], preferred_element_type=jnp.float32)
             sums = [0.0, 0.0, 0.0]
             for i in range(planes):
-                p = along[8 * i : 8 * i + 8]
+                p = along[16 * i : 16 * i + 16]
                 g = gxs[d, i : i + 1, at]
                 sums[0] += gxds[d, i : i + 1, at] * p
                 sums[1] += g * p
-                sums[2] += g * slope[8 * i : 8 * i + 8]
+                sums[2] += g * slope[16 * i : 16 * i + 16]
             y = gys[d, :, at]
             f = (y * sums[0], gyds[d, :, at] * sums[1], y * sums[2])
             for i in range(3):
@@ -430,7 +443,6 @@
         vel_out[i] = v
         pos_out[i] = loc[i] + timestep * v
     for d in range(1, na):
-        crd_copy(d).wait_send()
         fr_copy(d).wait_send()
     for c in sends:
         c.wait_send()
@@ -454,15 +466,15 @@
     thick, rows, depth = observed_volume_values.shape
     atoms = atom_locations.shape[2]
     members, bricks = lax.axis_size("replica"), lax.axis_size("brick")
-    na = members // 2
+    na = members // 4
     planes = thick + 2 * HALO
-    wide = planes * 8
+    wide = planes * 16
     cells = atoms // CELL
     blocks = cells + 5
     f32, bf16, i32 = jnp.float32, jnp.bfloat16, jnp.int32
     vmem = pl.BlockSpec(memory_space=pltpu.VMEM)
     hbm = pl.BlockSpec(memory_space=pltpu.HBM)
-    edge = 2 * HALO * 8
+    edge = 2 * HALO * 16
     scratch = [
         pltpu.VMEM((3, 1, atoms), f32),
         pltpu.VMEM((1, atoms), f32),
@@ -478,13 +490,14 @@
         pltpu.VMEM((na, depth, 2 * atoms), bf16),
         pltpu.VMEM((na, 16, atoms), f32),
         pltpu.VMEM((na, 16, atoms), f32),
-        pltpu.VMEM((na, 8, atoms), f32),
-        pltpu.VMEM((na, 8, atoms), f32),
+        pltpu.VMEM((na, 16, atoms), f32),
+        pltpu.VMEM((na, 16, atoms), f32),
         pltpu.VMEM((wide, depth), f32),
-        pltpu.VMEM((wide, depth), f32),
-        pltpu.VMEM((2, edge, depth), f32),
-        pltpu.VMEM((2, edge, depth), f32),
-        pltpu.VMEM((planes, 2, 2, 8, depth), f32),
+        pltpu.VMEM((wide, depth), bf16),
+        pltpu.VMEM((3, wide, depth), bf16),
+        pltpu.VMEM((4, edge, depth), bf16),
+        pltpu.VMEM((4, edge, depth), bf16),
+        pltpu.VMEM((planes, 2, 16, depth), f32),
         pltpu.VMEM((1, atoms), f32),
         pltpu.VMEM((1, atoms), f32),
         pltpu.VMEM((wide, depth), bf16),
@@ -504,7 +517,7 @@
         pltpu.VMEM((bricks, 1, CELL), f32),
         pltpu.SemaphoreType.DMA((15,)),
     ]
-    for count in (na, 2, 2, 1, 2, 2, na, bricks):
+    for count in (na, 2, 2, 4, 4, 4, na, bricks):
         scratch += [pltpu.SemaphoreType.DMA((count,))] * 2
     tall = lambda v: v.reshape(3, 1, atoms)
     new_positions, new_velocities, deviation = pl.pallas_call(

time: 53.2 us -> 46.6 us (0.88)
  Pallas kernels: 49.9 us -> 43.4 us
    pallas_call x1, Pallas kernels: 49.9 us -> 43.4 us  [local(): pl.pallas_call(functools.partial(kernel, (members, bricks, thick, rows, d...]
where the time goes in v4:
time: 46.6 us; the launch traced here: 46.5 us
  Pallas kernels  43.4 us (93%)
  local copies, waits for them, and re-layouts  1.8 us (4%)
  between operations  1.29 us (3%)
    pallas_call x1, Pallas kernels, local(): pl.pallas_call(functools.partial(kernel, (members, bricks, thick, rows, d...  43.4 us
    unnamed x3, local copies, waits for them, and re-layouts  1.8 us

profile of v4, /device:TPU:1, one launch (start us, length us, event | category | flops | bytes accessed | tf_op | source)
XLA Modules:
  0.0 46.5 jit_solution(9669115009992188126)
XLA Ops:
  1.3 43.4 %shard_map.148 = (f32[3,1,768]{2,1,0:T(1,128)S(1)}, f32[3,1,768]{2,1,0:T(1,128)S(1)}, f32[10,4,128]{2,1,0:T(4,128)S(1)}) custom-call(f32[3,1,768]{2,1,0:T(1,128)} %bitcast.6, f32[3,1,768]{2,1,0:T(1,128)} %bitcast.7, f32[768]{0:T(1024)} %mass_at.1, f32[768]{0:T(1024)} %load_at.1, f32[768]{0:T(1024)} %strength_at.1, f32[768]{0:T(1024)} %sigma_at.1, ...), custom_call_target="tpu_custom_call" | custom-call | flops 1200000000 | bytes 400000 | tf_op jit(solution)/shard_map/pallas_call | solution.py:523
  44.7 0.6 %copy.20 = f32[1,3,768]{2,0,1:T(1,128)} copy(f32[1,3,768]{2,0,1:T(1,128)S(1)} %bitcast.5) | data formatting | bytes 18432
  45.3 0.6 %copy.21 = f32[1,3,768]{2,0,1:T(1,128)} copy(f32[1,3,768]{2,0,1:T(1,128)S(1)} %bitcast.4) | data formatting | bytes 18432
  45.9 0.6 %copy.22 = f32[10,4,128]{2,1,0:T(4,128)} copy(f32[10,4,128]{2,1,0:T(4,128)S(1)} %get-tuple-element.14) | data formatting | bytes 40960

commit v5 on v4

--- a/solution.py
+++ b/solution.py
@@ -130,6 +130,10 @@
         dx, dp = B_STEPS[k]
         return ((x + dx) % 2) * half + zh * 2 + (zp + dp) % 2
 
+    def brick_at(n):
+        y, xh, core = n // 4, n // 2 % 2, n % 2
+        return (b // 4 + y) % (bricks // 4) * 4 + (b // 2 + xh) % 2 * 2 + (b + core) % 2
+
     def nearest(t):
         odd = t % 2
         return odd * ((t + 1) // 2) + (1 - odd) * ((na - t // 2) % na)
@@ -143,7 +147,7 @@
     barrier = pltpu.get_barrier_semaphore()
     partners = [a_peer(d) for d in direct]
     partners += [(b_rep(k), n) for k in range(1, 4) for n in (b, up, down)]
-    partners += [(r, (b + d) % bricks) for d in range(1, bricks)]
+    partners += [(r, brick_at(n)) for n in range(1, bricks)]
     for p in partners:
         pl.semaphore_signal(barrier, inc=1, device_id=p, device_id_type=MESH)
 
@@ -170,7 +174,25 @@
     }
     for c in copies.values():
         c.start()
-    for name in ("loc", "flag", "strength", "load", "sigma", "spots"):
+    copies["loc"].wait()
+    sends = []
+
+    def remote(src, dst, ss, rsem, device):
+        return pltpu.make_async_remote_copy(
+            src_ref=src, dst_ref=dst, send_sem=ss, recv_sem=rsem, device_id=device, device_id_type=MESH
+        )
+
+    def post(*a):
+        c = remote(*a)
+        c.start()
+        sends.append(c)
+        return c
+
+    pl.semaphore_wait(barrier, len(partners))
+    crd_in = {}
+    for d in reversed(direct):
+        crd_in[d] = post(crd.at[0], crd.at[d], crd_ss.at[d], crd_rs.at[d], a_peer(d))
+    for name in ("flag", "strength", "load", "sigma", "spots"):
         copies[name].wait()
     loc = crd.at[0]
     occ = flag_ref[...].astype(jnp.float32)
@@ -244,23 +266,6 @@
     for ref in (bx, bq, by, bz):
         ref[none] = jnp.zeros((1, CELL), ref.dtype)
 
-    sends = []
-
-    def remote(src, dst, ss, rsem, device):
-        return pltpu.make_async_remote_copy(
-            src_ref=src, dst_ref=dst, send_sem=ss, recv_sem=rsem, device_id=device, device_id_type=MESH
-        )
-
-    def post(*a):
-        c = remote(*a)
-        c.start()
-        sends.append(c)
-        return c
-
-    pl.semaphore_wait(barrier, len(partners))
-    crd_in = {}
-    for d in reversed(direct):
-        crd_in[d] = post(crd.at[0], crd.at[d], crd_ss.at[d], crd_rs.at[d], a_peer(d))
     gh_in = [
         post(gsend.at[0], glo, gh_ss.at[0], gh_rs.at[0], (r, up)),
         post(gsend.at[1], ghi, gh_ss.at[1], gh_rs.at[1], (r, down)),
@@ -299,11 +304,11 @@
     mine[...] = acc[...].astype(jnp.bfloat16)
     lower, upper = mine.at[pl.ds(0, edge)], mine.at[pl.ds(wide - edge, edge)]
     map_in = []
-    for k in (3, 2, 1, 0):
+    for k in (1, 3, 0, 2):
         map_in.append(post(upper, lo.at[k], lo_ss.at[k], lo_rs.at[k], (b_rep(k), up)))
         map_in.append(post(lower, hi.at[k], hi_ss.at[k], hi_rs.at[k], (b_rep(k), down)))
-        if k:
-            map_in.append(post(mine, rs.at[k - 1], rs_ss.at[k], rs_rs.at[k], (b_rep(k), b)))
+    for k in (3, 1, 2):
+        map_in.append(post(mine, rs.at[k - 1], rs_ss.at[k], rs_rs.at[k], (b_rep(k), b)))
 
     for c in gh_in:
         c.wait_recv()
@@ -428,7 +433,8 @@
         row = row + square[:, c * CELL : (c + 1) * CELL]
     kin[0] = row
     kn_in = [
-        post(kin.at[0], kin.at[d], kn_ss.at[d], kn_rs.at[d], (r, (b + d) % bricks)) for d in range(1, bricks)
+        post(kin.at[0], kin.at[n], kn_ss.at[n], kn_rs.at[n], (r, brick_at(n)))
+        for n in sorted(range(1, bricks), key=lambda n: -(min(n // 4, 4 - n // 4) + n // 2 % 2 * 2 + n % 2))
     ]
     for c in kn_in:
         c.wait_recv()
@@ -446,6 +452,15 @@
         fr_copy(d).wait_send()
     for c in sends:
         c.wait_send()
+
+
+def write(count, *refs):
+    sources, targets, sem = refs[:count], refs[count:-1], refs[-1]
+    copies = [pltpu.make_async_copy(a, c, sem.at[i]) for i, (a, c) in enumerate(zip(sources, targets))]
+    for c in copies:
+        c.start()
+    for c in copies:
+        c.wait()
 
 
 def local(
@@ -556,6 +571,14 @@
         pltpu.with_memory_space_constraint(observed_volume_values, pltpu.HBM),
         pltpu.with_memory_space_constraint(voxel_reciprocal_spread, pltpu.HBM),
     )
+    made = (new_positions, new_velocities, deviation)
+    new_positions, new_velocities, deviation = pl.pallas_call(
+        functools.partial(write, len(made)),
+        out_shape=tuple(jax.ShapeDtypeStruct(v.shape, v.dtype) for v in made),
+        in_specs=[vmem] * len(made),
+        out_specs=tuple(hbm for _ in made),
+        scratch_shapes=[pltpu.SemaphoreType.DMA((len(made),))],
+    )(*(pltpu.with_memory_space_constraint(v, pltpu.VMEM) for v in made))
     return (
         new_positions.reshape(1, 3, atoms),
         new_velocities.reshape(1, 3, atoms),

time: 46.6 us -> 46 us (0.987)
  local copies, waits for them, and re-layouts: 1.8 us -> 0 us
  Pallas kernels: 43.4 us -> 44.5 us
    unnamed x3 -> x0, local copies, waits for them, and re-layouts: 1.8 us -> none
    pallas_call x0 -> x1, Pallas kernels: none -> 0.64 us  [local(): pl.pallas_call(functools.partial(write, len(made)), out_shape=tuple((jax....]
    pallas_call x1, Pallas kernels: 43.4 us -> 43.9 us  [local(): pl.pallas_call(functools.partial(kernel, (members, bricks, thick, rows, d...]
where the time goes in v5:
time: 46 us; the launch traced here: 45.8 us
  Pallas kernels  44.5 us (97%)
  between operations  1.29 us (3%)
    pallas_call x1, Pallas kernels, local(): pl.pallas_call(functools.partial(kernel, (members, bricks, thick, rows, d...  43.9 us

profile of v5, /device:TPU:1, one launch (start us, length us, event | category | flops | bytes accessed | tf_op | source)
XLA Modules:
  0.0 45.8 jit_solution(17402233337629207322)
XLA Ops:
  1.3 43.9 %shard_map.148 = (f32[3,1,768]{2,1,0:T(1,128)S(1)}, f32[3,1,768]{2,1,0:T(1,128)S(1)}, f32[10,4,128]{2,1,0:T(4,128)S(1)}) custom-call(f32[3,1,768]{2,1,0:T(1,128)} %bitcast.4, f32[3,1,768]{2,1,0:T(1,128)} %bitcast.5, f32[768]{0:T(1024)} %mass_at.1, f32[768]{0:T(1024)} %load_at.1, f32[768]{0:T(1024)} %strength_at.1, f32[768]{0:T(1024)} %sigma_at.1, ...), custom_call_target="tpu_custom_call" | custom-call | flops 1200000000 | bytes 400000 | tf_op jit(solution)/shard_map/pallas_call | solution.py:538
  45.2 0.6 %shard_map.149 = (f32[3,1,768]{2,1,0:T(1,128)}, f32[3,1,768]{2,1,0:T(1,128)}, f32[10,4,128]{2,1,0:T(4,128)}) custom-call(f32[3,1,768]{2,1,0:T(1,128)S(1)} %get-tuple-element.9.refs_0_, f32[3,1,768]{2,1,0:T(1,128)S(1)} %get-tuple-element.10.refs_1_, f32[10,4,128]{2,1,0:T(4,128)S(1)} %get-tuple-element.11.refs_2_), custom_call_target="tpu_custom_call" | custom-call | tf_op jit(solution)/shard_map/pallas_call | solution.py:575

commit v6 on v5

--- a/solution.py
+++ b/solution.py
@@ -45,7 +45,7 @@
     spots_at,
     lists_at,
     tally_at,
-    warm_at,
+    warm,
     obs,
     vrs,
     pos_out,
@@ -60,7 +60,6 @@
     spots,
     lists,
     tally,
-    warm,
     crd,
     zz,
     gxs,
@@ -134,6 +133,10 @@
         y, xh, core = n // 4, n // 2 % 2, n % 2
         return (b // 4 + y) % (bricks // 4) * 4 + (b // 2 + xh) % 2 * 2 + (b + core) % 2
 
+    far_first = sorted(
+        range(1, bricks), key=lambda n: -(min(n // 4, 4 - n // 4) + n // 2 % 2 * 2 + n % 2)
+    )
+
     def nearest(t):
         odd = t % 2
         return odd * ((t + 1) // 2) + (1 - odd) * ((na - t // 2) % na)
@@ -145,9 +148,9 @@
         relayed = {1: (3, 2), 7: (5, 6), 2: (4, 2)}
 
     barrier = pltpu.get_barrier_semaphore()
-    partners = [a_peer(d) for d in direct]
-    partners += [(b_rep(k), n) for k in range(1, 4) for n in (b, up, down)]
-    partners += [(r, brick_at(n)) for n in range(1, bricks)]
+    partners = [a_peer(d) for d in reversed(direct)]
+    partners += [(r, brick_at(n)) for n in far_first]
+    partners += [(b_rep(k), n) for n in (up, down, b) for k in range(1, 4)]
     for p in partners:
         pl.semaphore_signal(barrier, inc=1, device_id=p, device_id_type=MESH)
 
@@ -162,7 +165,6 @@
         "tally": (tally_at, tally),
         "vel": (vel_at, vel),
         "mass": (mass_at, mass_ref.at[0]),
-        "warm": (warm_at, warm),
     }
     for t in range(2):
         tile = pl.ds(pl.multiple_of(t * (rows // 2) + zh * 8, 8), 8)
@@ -188,10 +190,6 @@
         sends.append(c)
         return c
 
-    pl.semaphore_wait(barrier, len(partners))
-    crd_in = {}
-    for d in reversed(direct):
-        crd_in[d] = post(crd.at[0], crd.at[d], crd_ss.at[d], crd_rs.at[d], a_peer(d))
     for name in ("flag", "strength", "load", "sigma", "spots"):
         copies[name].wait()
     loc = crd.at[0]
@@ -249,23 +247,10 @@
 
     spread(0)
 
-    for c in range(cells):
-        at = slice(c * CELL, (c + 1) * CELL)
-        for i, col in enumerate((colx, coly, colz)):
-            v = jnp.broadcast_to(loc[i, :, at], (CELL, CELL)).T
-            col[at] = v * 2.0**shift_z if i == 0 else fixed(v, (rows, depth)[i - 1])
-
-    scale_x = 2.0**shift_z
-    for c in range(cells):
-        at = slice(c * CELL, (c + 1) * CELL)
-        bx[c] = loc[0, :, at] * scale_x
-        by[c] = fixed(loc[1, :, at], rows)
-        bz[c] = fixed(loc[2, :, at], depth)
-        bq[c] = q[:, at]
-    none = cells + 4
-    for ref in (bx, bq, by, bz):
-        ref[none] = jnp.zeros((1, CELL), ref.dtype)
-
+    pl.semaphore_wait(barrier, len(partners))
+    crd_in = {}
+    for d in reversed(direct):
+        crd_in[d] = post(crd.at[0], crd.at[d], crd_ss.at[d], crd_rs.at[d], a_peer(d))
     gh_in = [
         post(gsend.at[0], glo, gh_ss.at[0], gh_rs.at[0], (r, up)),
         post(gsend.at[1], ghi, gh_ss.at[1], gh_rs.at[1], (r, down)),
@@ -284,6 +269,24 @@
         ),
     ]
 
+
+    for c in range(cells):
+        at = slice(c * CELL, (c + 1) * CELL)
+        for i, col in enumerate((colx, coly, colz)):
+            v = jnp.broadcast_to(loc[i, :, at], (CELL, CELL)).T
+            col[at] = v * 2.0**shift_z if i == 0 else fixed(v, (rows, depth)[i - 1])
+
+    scale_x = 2.0**shift_z
+    for c in range(cells):
+        at = slice(c * CELL, (c + 1) * CELL)
+        bx[c] = loc[0, :, at] * scale_x
+        by[c] = fixed(loc[1, :, at], rows)
+        bz[c] = fixed(loc[2, :, at], depth)
+        bq[c] = q[:, at]
+    none = cells + 4
+    for ref in (bx, bq, by, bz):
+        ref[none] = jnp.zeros((1, CELL), ref.dtype)
+
     def await_crd(d):
         crd_in[d].wait_recv()
         if d in relayed:
@@ -291,7 +294,7 @@
             crd_in[far] = post(crd.at[d], crd.at[far], crd_ss.at[far], crd_rs.at[far], a_peer(to))
 
     if na == 8:
-        for ready, then in (((1, 7), (1,)), ((2,), (7, 2)), ((6,), (6,)), ((3,), (3,)), ((5,), (5,)), ((4,), (4,))):
+        for ready, then in (((1, 7, 2), (1, 7, 2)), ((6,), (6,)), ((3,), (3,)), ((5,), (5,)), ((4,), (4,))):
             for d in ready:
                 await_crd(d)
             for d in then:
@@ -405,7 +408,7 @@
     lax.fori_loop(0, na, give, 0)
 
     lax.fori_loop(units // 2, units, pair, 0)
-    for name in ("vel", "mass", "warm"):
+    for name in ("vel", "mass"):
         copies[name].wait()
     mass = mass_ref[...]
     light = timestep / mass
@@ -434,7 +437,7 @@
     kin[0] = row
     kn_in = [
         post(kin.at[0], kin.at[n], kn_ss.at[n], kn_rs.at[n], (r, brick_at(n)))
-        for n in sorted(range(1, bricks), key=lambda n: -(min(n // 4, 4 - n // 4) + n // 2 % 2 * 2 + n % 2))
+        for n in far_first
     ]
     for c in kn_in:
         c.wait_recv()
@@ -442,7 +445,7 @@
         row = row + kin[d]
     kinetic = jnp.sum(row, axis=1, keepdims=True)
     present = kinetic / (3 * atoms * bricks * boltzmann) + 1e-06
-    wanted = jnp.full((1, 1), warm[0].astype(jnp.float32))
+    wanted = jnp.full((1, 1), warm[0, 0].astype(jnp.float32))
     ratio = jnp.sqrt(1.0 + heat_bath_damping * (wanted / present - 1.0))
     for i in range(3):
         v = ratio * v_half[i]
@@ -489,6 +492,7 @@
     f32, bf16, i32 = jnp.float32, jnp.bfloat16, jnp.int32
     vmem = pl.BlockSpec(memory_space=pltpu.VMEM)
     hbm = pl.BlockSpec(memory_space=pltpu.HBM)
+    smem = pl.BlockSpec(memory_space=pltpu.SMEM)
     edge = 2 * HALO * 16
     scratch = [
         pltpu.VMEM((3, 1, atoms), f32),
@@ -500,7 +504,6 @@
         pltpu.VMEM((2, GHOST), i32),
         pltpu.SMEM(paired_partner_lists.shape, i32),
         pltpu.SMEM((cells,), i32),
-        pltpu.SMEM((1,), i32),
         pltpu.VMEM((na, 3, 1, atoms), f32),
         pltpu.VMEM((na, depth, 2 * atoms), bf16),
         pltpu.VMEM((na, 16, atoms), f32),
@@ -530,7 +533,7 @@
         pltpu.VMEM((atoms, CELL), i32),
         pltpu.VMEM((3, atoms, CELL), f32),
         pltpu.VMEM((bricks, 1, CELL), f32),
-        pltpu.SemaphoreType.DMA((15,)),
+        pltpu.SemaphoreType.DMA((14,)),
     ]
     for count in (na, 2, 2, 4, 4, 4, na, bricks):
         scratch += [pltpu.SemaphoreType.DMA((count,))] * 2
@@ -542,7 +545,7 @@
             jax.ShapeDtypeStruct((3, 1, atoms), f32),
             jax.ShapeDtypeStruct((thick, rows // members, depth), f32),
         ),
-        in_specs=[hbm] * 13,
+        in_specs=[hbm] * 10 + [smem] + [hbm] * 2,
         out_specs=(vmem, vmem, vmem),
         scratch_shapes=scratch,
         compiler_params=pltpu.CompilerParams(
@@ -567,7 +570,7 @@
                 cell_usage_tally,
             )
         ),
-        target_warmth_levels,
+        target_warmth_levels.reshape(1, 1),
         pltpu.with_memory_space_constraint(observed_volume_values, pltpu.HBM),
         pltpu.with_memory_space_constraint(voxel_reciprocal_spread, pltpu.HBM),
     )

time: 46 us -> 45.3 us (0.985)
  Pallas kernels: 44.5 us -> 43.9 us
    pallas_call x1, Pallas kernels: 43.9 us -> 43.2 us  [local(): pl.pallas_call(functools.partial(kernel, (members, bricks, thick, rows, d...]
where the time goes in v6:
time: 45.3 us; the launch traced here: 45.2 us
  Pallas kernels  43.9 us (97%)
  between operations  1.29 us (3%)
    pallas_call x1, Pallas kernels, local(): pl.pallas_call(functools.partial(kernel, (members, bricks, thick, rows, d...  43.2 us

profile of v6, /device:TPU:1, one launch (start us, length us, event | category | flops | bytes accessed | tf_op | source)
XLA Modules:
  0.0 45.2 jit_solution(17730793872793933999)
XLA Ops:
  1.3 43.2 %shard_map.148 = (f32[3,1,768]{2,1,0:T(1,128)S(1)}, f32[3,1,768]{2,1,0:T(1,128)S(1)}, f32[10,4,128]{2,1,0:T(4,128)S(1)}) custom-call(f32[3,1,768]{2,1,0:T(1,128)} %bitcast.6, f32[3,1,768]{2,1,0:T(1,128)} %bitcast.7, f32[768]{0:T(1024)} %mass_at.1, f32[768]{0:T(1024)} %load_at.1, f32[768]{0:T(1024)} %strength_at.1, f32[768]{0:T(1024)} %sigma_at.1, ...), custom_call_target="tpu_custom_call" | custom-call | flops 1200000000 | bytes 400000 | tf_op jit(solution)/shard_map/pallas_call | solution.py:541
  44.5 0.6 %shard_map.149 = (f32[3,1,768]{2,1,0:T(1,128)}, f32[3,1,768]{2,1,0:T(1,128)}, f32[10,4,128]{2,1,0:T(4,128)}) custom-call(f32[3,1,768]{2,1,0:T(1,128)S(1)} %get-tuple-element.9.refs_0_, f32[3,1,768]{2,1,0:T(1,128)S(1)} %get-tuple-element.10.refs_1_, f32[10,4,128]{2,1,0:T(4,128)S(1)} %get-tuple-element.11.refs_2_), custom_call_target="tpu_custom_call" | custom-call | tf_op jit(solution)/shard_map/pallas_call | solution.py:578

commit v7 on v6

--- a/solution.py
+++ b/solution.py
@@ -69,8 +69,7 @@
     acc,
     mine,
     rs,
-    lo,
-    hi,
+    halo,
     obv,
     amps,
     ivs,
@@ -98,10 +97,8 @@
     ob_rs,
     rs_ss,
     rs_rs,
-    lo_ss,
-    lo_rs,
-    hi_ss,
-    hi_rs,
+    hl_ss,
+    hl_rs,
     fr_ss,
     fr_rs,
     kn_ss,
@@ -240,7 +237,7 @@
         zz[d, :, :atoms] = gzb
         left = (amp * gx)[:planes, None, :] * gy[None]
         part = dot_t(left.reshape(wide, atoms).astype(jnp.bfloat16), gzb)
-        if d == 0:
+        if isinstance(d, int):
             acc[...] = part
         else:
             acc[...] += part
@@ -270,11 +267,14 @@
     ]
 
 
-    for c in range(cells):
-        at = slice(c * CELL, (c + 1) * CELL)
+    def column(c, _):
+        at = pl.ds(pl.multiple_of(c * CELL, CELL), CELL)
         for i, col in enumerate((colx, coly, colz)):
             v = jnp.broadcast_to(loc[i, :, at], (CELL, CELL)).T
             col[at] = v * 2.0**shift_z if i == 0 else fixed(v, (rows, depth)[i - 1])
+        return 0
+
+    lax.fori_loop(0, cells, column, 0)
 
     scale_x = 2.0**shift_z
     for c in range(cells):
@@ -293,25 +293,56 @@
             far, to = relayed[d]
             crd_in[far] = post(crd.at[d], crd.at[far], crd_ss.at[far], crd_rs.at[far], a_peer(to))
 
-    if na == 8:
-        for ready, then in (((1, 7, 2), (1, 7, 2)), ((6,), (6,)), ((3,), (3,)), ((5,), (5,)), ((4,), (4,))):
-            for d in ready:
-                await_crd(d)
-            for d in then:
-                spread(d)
-    else:
-        for d in direct:
-            await_crd(d)
-            spread(d)
+    early = (1, 7, 2) if na == 8 else ()
+    for d in early:
+        await_crd(d)
+
+    def collect(t, _):
+        d = nearest(t)
+
+        @pl.when(t > len(early))
+        def _():
+            remote(crd.at[0], crd.at[d], crd_ss.at[d], crd_rs.at[d], a_peer(d)).wait_recv()
+
+        spread(d)
+        return 0
+
+    lax.fori_loop(1, na, collect, 0)
 
     mine[...] = acc[...].astype(jnp.bfloat16)
-    lower, upper = mine.at[pl.ds(0, edge)], mine.at[pl.ds(wide - edge, edge)]
+    core = b % 2
+
+    def post_edge(side, k):
+        start = pl.multiple_of((1 - side) * (wide - edge), 16)
+        at = side * 4 + k
+        post(
+            mine.at[pl.ds(start, edge)],
+            halo.at[side, k],
+            hl_ss.at[at],
+            hl_rs.at[at],
+            (b_rep(k), (b + bricks + 1 - 2 * side) % bricks),
+        )
+
     map_in = []
-    for k in (1, 3, 0, 2):
-        map_in.append(post(upper, lo.at[k], lo_ss.at[k], lo_rs.at[k], (b_rep(k), up)))
-        map_in.append(post(lower, hi.at[k], hi_ss.at[k], hi_rs.at[k], (b_rep(k), down)))
-    for k in (3, 1, 2):
+
+    def post_map(k):
         map_in.append(post(mine, rs.at[k - 1], rs_ss.at[k], rs_rs.at[k], (b_rep(k), b)))
+
+    for k in (1, 0, 3, 2):
+        post_edge(1 - core, k)
+    post_map(3)
+    for k in (3, 1):
+        post_edge(core, k)
+    post_map(1)
+    post_edge(core, 2)
+    post_map(2)
+    post_edge(core, 0)
+    for side in range(2):
+        for k in range(4):
+            at = side * 4 + k
+            map_in.append(
+                remote(mine.at[pl.ds(0, edge)], halo.at[side, k], hl_ss.at[at], hl_rs.at[at], (b_rep(k), up))
+            )
 
     for c in gh_in:
         c.wait_recv()
@@ -360,8 +391,9 @@
         c.wait_recv()
     wider = lambda v: v.astype(jnp.float32)
     total = acc[...] + wider(rs[0]) + wider(rs[1]) + wider(rs[2])
-    low = wider(lo[0]) + wider(lo[1]) + wider(lo[2]) + wider(lo[3])
-    high = wider(hi[0]) + wider(hi[1]) + wider(hi[2]) + wider(hi[3])
+    low, high = (
+        wider(halo[i, 0]) + wider(halo[i, 1]) + wider(halo[i, 2]) + wider(halo[i, 3]) for i in range(2)
+    )
     total = jnp.concatenate(
         [total[:edge] + low, total[edge : wide - edge], total[wide - edge :] + high], axis=0
     ).reshape(planes, 16, depth)
@@ -513,8 +545,7 @@
         pltpu.VMEM((wide, depth), f32),
         pltpu.VMEM((wide, depth), bf16),
         pltpu.VMEM((3, wide, depth), bf16),
-        pltpu.VMEM((4, edge, depth), bf16),
-        pltpu.VMEM((4, edge, depth), bf16),
+        pltpu.VMEM((2, 4, edge, depth), bf16),
         pltpu.VMEM((planes, 2, 16, depth), f32),
         pltpu.VMEM((1, atoms), f32),
         pltpu.VMEM((1, atoms), f32),
@@ -535,7 +566,7 @@
         pltpu.VMEM((bricks, 1, CELL), f32),
         pltpu.SemaphoreType.DMA((14,)),
     ]
-    for count in (na, 2, 2, 4, 4, 4, na, bricks):
+    for count in (na, 2, 2, 4, 8, na, bricks):
         scratch += [pltpu.SemaphoreType.DMA((count,))] * 2
     tall = lambda v: v.reshape(3, 1, atoms)
     new_positions, new_velocities, deviation = pl.pallas_call(

time: 45.3 us -> 44.8 us (0.989)
  Pallas kernels: 43.9 us -> 43.3 us
    pallas_call x1, Pallas kernels: 43.2 us -> 42.7 us  [local(): pl.pallas_call(functools.partial(kernel, (members, bricks, thick, rows, d...]
where the time goes in v7:
time: 44.8 us; the launch traced here: 44.6 us
  Pallas kernels  43.3 us (97%)
  between operations  1.29 us (3%)
    pallas_call x1, Pallas kernels, local(): pl.pallas_call(functools.partial(kernel, (members, bricks, thick, rows, d...  42.7 us

profile of v7, /device:TPU:1, one launch (start us, length us, event | category | flops | bytes accessed | tf_op | source)
XLA Modules:
  0.0 44.6 jit_solution(7277365775787702932)
XLA Ops:
  1.3 42.7 %shard_map.148 = (f32[3,1,768]{2,1,0:T(1,128)S(1)}, f32[3,1,768]{2,1,0:T(1,128)S(1)}, f32[10,4,128]{2,1,0:T(4,128)S(1)}) custom-call(f32[3,1,768]{2,1,0:T(1,128)} %bitcast.6, f32[3,1,768]{2,1,0:T(1,128)} %bitcast.7, f32[768]{0:T(1024)} %mass_at.1, f32[768]{0:T(1024)} %load_at.1, f32[768]{0:T(1024)} %strength_at.1, f32[768]{0:T(1024)} %sigma_at.1, ...), custom_call_target="tpu_custom_call" | custom-call | flops 1200000000 | bytes 400000 | tf_op jit(solution)/shard_map/pallas_call | solution.py:572
  43.9 0.6 %shard_map.149 = (f32[3,1,768]{2,1,0:T(1,128)}, f32[3,1,768]{2,1,0:T(1,128)}, f32[10,4,128]{2,1,0:T(4,128)}) custom-call(f32[3,1,768]{2,1,0:T(1,128)S(1)} %get-tuple-element.9.refs_0_, f32[3,1,768]{2,1,0:T(1,128)S(1)} %get-tuple-element.10.refs_1_, f32[10,4,128]{2,1,0:T(4,128)S(1)} %get-tuple-element.11.refs_2_), custom_call_target="tpu_custom_call" | custom-call | tf_op jit(solution)/shard_map/pallas_call | solution.py:609

commit v8 on v7

--- a/solution.py
+++ b/solution.py
@@ -147,7 +147,7 @@
     barrier = pltpu.get_barrier_semaphore()
     partners = [a_peer(d) for d in reversed(direct)]
     partners += [(r, brick_at(n)) for n in far_first]
-    partners += [(b_rep(k), n) for n in (up, down, b) for k in range(1, 4)]
+    partners += [(b_rep(k), b) for k in range(1, 4)]
     for p in partners:
         pl.semaphore_signal(barrier, inc=1, device_id=p, device_id_type=MESH)
 
@@ -310,6 +310,9 @@
     lax.fori_loop(1, na, collect, 0)
 
     mine[...] = acc[...].astype(jnp.bfloat16)
+    for c in gh_in:
+        c.wait_recv()
+
     core = b % 2
 
     def post_edge(side, k):
@@ -344,8 +347,6 @@
                 remote(mine.at[pl.ds(0, edge)], halo.at[side, k], hl_ss.at[at], hl_rs.at[at], (b_rep(k), up))
             )
 
-    for c in gh_in:
-        c.wait_recv()
     period_x = float(thick * bricks)
     for side, src in enumerate((glo, ghi)):
         if side == 0:

time: 44.8 us -> 44.8 us (level)
  no operation moved by 1% of the time
where the time goes in v8:
time: 44.8 us; the launch traced here: 44.6 us
  Pallas kernels  43.3 us (97%)
  between operations  1.29 us (3%)
    pallas_call x1, Pallas kernels, local(): pl.pallas_call(functools.partial(kernel, (members, bricks, thick, rows, d...  42.7 us

profile of v8, /device:TPU:1, one launch (start us, length us, event | category | flops | bytes accessed | tf_op | source)
XLA Modules:
  0.0 44.6 jit_solution(13260843127143618800)
XLA Ops:
  1.3 42.7 %shard_map.148 = (f32[3,1,768]{2,1,0:T(1,128)S(1)}, f32[3,1,768]{2,1,0:T(1,128)S(1)}, f32[10,4,128]{2,1,0:T(4,128)S(1)}) custom-call(f32[3,1,768]{2,1,0:T(1,128)} %bitcast.6, f32[3,1,768]{2,1,0:T(1,128)} %bitcast.7, f32[768]{0:T(1024)} %mass_at.1, f32[768]{0:T(1024)} %load_at.1, f32[768]{0:T(1024)} %strength_at.1, f32[768]{0:T(1024)} %sigma_at.1, ...), custom_call_target="tpu_custom_call" | custom-call | flops 1200000000 | bytes 400000 | tf_op jit(solution)/shard_map/pallas_call | solution.py:573
  44.0 0.6 %shard_map.149 = (f32[3,1,768]{2,1,0:T(1,128)}, f32[3,1,768]{2,1,0:T(1,128)}, f32[10,4,128]{2,1,0:T(4,128)}) custom-call(f32[3,1,768]{2,1,0:T(1,128)S(1)} %get-tuple-element.9.refs_0_, f32[3,1,768]{2,1,0:T(1,128)S(1)} %get-tuple-element.10.refs_1_, f32[10,4,128]{2,1,0:T(4,128)S(1)} %get-tuple-element.11.refs_2_), custom_call_target="tpu_custom_call" | custom-call | tf_op jit(solution)/shard_map/pallas_call | solution.py:610

commit v9 on v8

--- a/solution.py
+++ b/solution.py
@@ -401,9 +401,6 @@
     dev = total / members - obv[:, 0]
     grad = (restraint * obv[:, 1] * dev).astype(jnp.bfloat16)
     grd[...] = grad.reshape(wide, depth)
-    own = dev[HALO : HALO + thick]
-    own = jnp.where(x == 0, own[:, :8], own[:, 8:])
-    dev_out[...] = jnp.where(zp == 0, own[:, :share], own[:, share:])
 
     lanes = 256
 
@@ -440,6 +437,10 @@
 
     lax.fori_loop(0, na, give, 0)
 
+    own = dev[HALO : HALO + thick]
+    own = jnp.where(x == 0, own[:, :8], own[:, 8:])
+    dev_out[...] = jnp.where(zp == 0, own[:, :share], own[:, share:])
+
     lax.fori_loop(units // 2, units, pair, 0)
     for name in ("vel", "mass"):
         copies[name].wait()
@@ -454,14 +455,13 @@
         ]
         v_half.append(vel[i] + gain * jnp.concatenate(line, axis=1))
 
-    for d in range(1, na):
+    forces = [frc[0, i] for i in range(3)]
+    for d in (nearest(t) for t in range(1, na)):
         fr_copy(d).wait_recv()
+        forces = [f + frcin[d, i] for i, f in enumerate(forces)]
     square = jnp.zeros((1, atoms), jnp.float32)
     for i in range(3):
-        f = frc[0, i]
-        for d in range(1, na):
-            f = f + frcin[d, i]
-        v_half[i] = v_half[i] - push * f
+        v_half[i] = v_half[i] - push * forces[i]
         square = square + v_half[i] * v_half[i]
     square = mass * square
     row = square[:, :CELL]

time: 44.8 us -> 44.8 us (level)
  no operation moved by 1% of the time
where the time goes in v9:
time: 44.8 us; the launch traced here: 44.6 us
  Pallas kernels  43.3 us (97%)
  between operations  1.29 us (3%)
    pallas_call x1, Pallas kernels, local(): pl.pallas_call(functools.partial(kernel, (members, bricks, thick, rows, d...  42.7 us

profile of v9, /device:TPU:1, one launch (start us, length us, event | category | flops | bytes accessed | tf_op | source)
XLA Modules:
  0.0 44.6 jit_solution(14709181600946993676)
XLA Ops:
  1.3 42.7 %shard_map.148 = (f32[3,1,768]{2,1,0:T(1,128)S(1)}, f32[3,1,768]{2,1,0:T(1,128)S(1)}, f32[10,4,128]{2,1,0:T(4,128)S(1)}) custom-call(f32[3,1,768]{2,1,0:T(1,128)} %bitcast.6, f32[3,1,768]{2,1,0:T(1,128)} %bitcast.7, f32[768]{0:T(1024)} %mass_at.1, f32[768]{0:T(1024)} %load_at.1, f32[768]{0:T(1024)} %strength_at.1, f32[768]{0:T(1024)} %sigma_at.1, ...), custom_call_target="tpu_custom_call" | custom-call | flops 1200000000 | bytes 400000 | tf_op jit(solution)/shard_map/pallas_call | solution.py:573
  43.9 0.6 %shard_map.149 = (f32[3,1,768]{2,1,0:T(1,128)}, f32[3,1,768]{2,1,0:T(1,128)}, f32[10,4,128]{2,1,0:T(4,128)}) custom-call(f32[3,1,768]{2,1,0:T(1,128)S(1)} %get-tuple-element.9.refs_0_, f32[3,1,768]{2,1,0:T(1,128)S(1)} %get-tuple-element.10.refs_1_, f32[10,4,128]{2,1,0:T(4,128)S(1)} %get-tuple-element.11.refs_2_), custom_call_target="tpu_custom_call" | custom-call | tf_op jit(solution)/shard_map/pallas_call | solution.py:610
